TPU v7x, 512 devices: a whole 4x4x16 slice. The times are simulated.
512 devices in a mesh: group: 4 (over z_hi), dp: 32 (over y, z_lo, core), tensor: 4 (over x).
Axes of the slice: x: 4, y: 4, z: 16 (z_hi: 4, z_lo: 4; z = z_hi * 4 + z_lo), core: 2. Of those that a mesh axis runs over, the one named last changes fastest.
Arguments:
- queries: bfloat16 [16384, 4096], P(('group', 'dp'), 'tensor'), may hold values from -16 to 16
- span_state: bfloat16 [16384, 4096], P(('group', 'dp'), 'tensor'), may hold values from -6 to 6
- neigh_state: bfloat16 [65536, 4096], P(('group', 'dp'), 'tensor'), may hold values from -24 to 24
- counts: int32 [4, 64], P('group'), may hold values from 1 to 2
- norm_gain: float32 [4096], P('tensor'), may hold values from 0.5 to 1.5
- head_gate: float32 [32], P('tensor'), may hold values from 0.3 to 1.5
- out_grad: bfloat16 [16384, 4096], P(('group', 'dp'), 'tensor'), may hold values from -6 to 6
Outputs:
- cross_output: bfloat16 [16384, 4096], P(('group', 'dp'), 'tensor')
- query_grad: bfloat16 [16384, 4096], P(('group', 'dp'), 'tensor')
- span_grad: bfloat16 [16384, 4096], P(('group', 'dp'), 'tensor')
- neighbour_grad: bfloat16 [65536, 4096], P(('group', 'dp'), 'tensor')
- gate_grad: float32 [32], P('tensor')
Inputs may be any that keep to these rules, and one draw needn't show every extreme that they name: Slot j of span c holds a retrieved neighbour exactly when j < counts[c].
All inputs are finite; a program needn't handle non-finite values.
Results may differ from a plain program's by a relative error of at most 0.0095.
The roundings to bfloat16 on the way count: a program that leaves them out, or rounds other values in their place, can miss the bound.
Values may be sent and summed in bfloat16 or wider, within the bound.
No kernel may reach another device: no remote copies, remote signals or barrier semaphores. Data moves between devices by JAX's collectives and lax.ppermute only.
A program may use at most 64 MiB of HBM per device.

v0:
```python
import math

import jax
import jax.numpy as jnp
from jax import lax
from jax.sharding import PartitionSpec as P

CH = 64
NB = 2
NL = 128


epsilon = 1e-05
masked_score = -1e30


def shifted(value, axis, steps):
    count = lax.axis_size(axis)
    leading, last = (max(0, -steps), min(count, count - steps))
    return lax.ppermute(value, axis, [(source, source + steps) for source in range(leading, last)])


def product(form, left, right):
    return jnp.einsum(form, left, right, preferred_element_type=jnp.float32)


def encoder_forward(normed, neighbours, contexts):
    slot_count = normed.shape[1]
    spread = jnp.broadcast_to(
        contexts[:, None], (contexts.shape[0], slot_count) + contexts.shape[1:]
    )
    all_keys = jnp.concatenate([normed, spread], axis=2)
    scores = product("cjqhd,cjkhd->cjhqk", normed, all_keys) / normed.shape[-1]
    powers = jnp.exp(scores)
    weights = powers / jnp.sum(powers, axis=-1, keepdims=True)
    rounded = weights.astype(jnp.bfloat16)
    mixture = product("cjhqk,cjkhd->cjqhd", rounded, all_keys)
    encoded = (neighbours.astype(jnp.float32) + mixture).astype(jnp.bfloat16)
    return (encoded, (all_keys, weights, rounded, mixture))


def encoder_backward(grad_encoded, normed, saved):
    all_keys, weights, rounded, mixture = saved
    grad_rounded = grad_encoded.astype(jnp.bfloat16)
    grad_weights = product("cjqhd,cjkhd->cjhqk", grad_rounded, all_keys)
    offset = jnp.moveaxis(jnp.sum(grad_encoded * mixture, axis=-1), -1, 2)[..., None]
    score_grad = (weights * (grad_weights - offset) / normed.shape[-1]).astype(jnp.bfloat16)
    normed_grad = product("cjhqk,cjkhd->cjqhd", score_grad, all_keys)
    key_grad = product("cjhqk,cjqhd->cjkhd", score_grad, normed) + product(
        "cjhqk,cjqhd->cjkhd", rounded, grad_rounded
    )
    length = normed.shape[2]
    normed_grad = normed_grad + key_grad[:, :, :length]
    context_grad = jnp.sum(key_grad[:, :, length:], axis=1)
    return (normed_grad, context_grad)


def cross_attend(blocks, grad_blocks, keys, usable, present, gate_tanh):
    scale = 1.0 / math.sqrt(blocks.shape[-1])
    scores = product("brhd,bmhd->bhrm", blocks, keys) * scale
    scores = jnp.where(usable[:, None, None, :], scores, masked_score)
    highest = jnp.max(scores, axis=-1, keepdims=True)
    powers = jnp.exp(scores - highest)
    weights = powers / jnp.sum(powers, axis=-1, keepdims=True)
    rounded = weights.astype(jnp.bfloat16)
    attended = product("bhrm,bmhd->brhd", rounded, keys)
    present_mask = present[:, None, None, None]
    attended = jnp.where(present_mask, attended, 0.0)
    output = (gate_tanh[:, None] * attended).astype(jnp.bfloat16)
    grad_output = grad_blocks.astype(jnp.float32)
    gate_term = jnp.sum(grad_output * attended, axis=(0, 1, 3))
    att_grad = jnp.where(present_mask, gate_tanh[:, None] * grad_output, 0.0)
    grad_rounded = att_grad.astype(jnp.bfloat16)
    grad_weights = product("brhd,bmhd->bhrm", grad_rounded, keys)
    offset = jnp.moveaxis(jnp.sum(att_grad * attended, axis=-1), -1, 1)[..., None]
    score_grad = (weights * (grad_weights - offset) * scale).astype(jnp.bfloat16)
    query_grad = product("bhrm,bmhd->brhd", score_grad, keys).astype(jnp.bfloat16)
    key_grad = product("bhrm,brhd->bmhd", score_grad, blocks) + product(
        "bhrm,brhd->bmhd", rounded, grad_rounded
    )
    return (output, query_grad, key_grad, gate_term)


def shards(queries, span_state, neigh_state, counts, norm_gain, head_gate, out_grad):
    head_count = head_gate.shape[0]
    local_width = queries.shape[1]
    head_dim = local_width // head_count
    row_count = queries.shape[0]
    span_count = row_count // CH
    seq_spans = counts.shape[1]
    lead = CH - 1

    def blockify(matrix):
        return matrix.reshape(-1, CH, head_count, head_dim)

    neighbours = neigh_state.reshape(span_count, NB, NL, head_count, head_dim)
    contexts = span_state.reshape(span_count, CH, head_count, head_dim)
    gains = norm_gain.reshape(head_count, head_dim)
    floats = neighbours.astype(jnp.float32)
    square_sum = lax.psum(jnp.sum(floats * floats, axis=(3, 4)), "tensor")
    full_width = lax.axis_size("tensor") * local_width
    inverse = lax.rsqrt(square_sum / full_width + epsilon)[..., None, None]
    scaled = floats * inverse
    normed = (scaled * gains).astype(jnp.bfloat16)
    encoded, saved = encoder_forward(normed, neighbours, contexts)
    line_index = lax.axis_index("dp")
    first_span = line_index * span_count
    flat_counts = counts.reshape(-1)
    own_counts = lax.dynamic_slice_in_dim(flat_counts, first_span, span_count)
    gate_tanh = jnp.tanh(head_gate)
    usable = jnp.repeat(jnp.arange(NB)[None, :] < own_counts[:, None], NL, axis=1)
    present = own_counts > 0
    keys = encoded.reshape(span_count, NB * NL, head_count, head_dim)
    kept = row_count - lead
    padding = jnp.zeros((lead, local_width), jnp.bfloat16)
    blocks = blockify(jnp.concatenate([queries[lead:], padding], axis=0))
    grad_blocks = blockify(jnp.concatenate([out_grad[lead:], padding], axis=0))
    earlier_keys = shifted(keys[span_count - 1], "dp", 1)
    earlier_count = lax.dynamic_index_in_dim(
        flat_counts, jnp.maximum(first_span - 1, 0), keepdims=False
    )
    earlier_present = jnp.logical_and(first_span % seq_spans > 0, earlier_count > 0)
    earlier_usable = jnp.repeat(jnp.arange(NB) < earlier_count, NL)
    front_row = jnp.zeros((1, local_width), jnp.bfloat16)
    first_block = blockify(jnp.concatenate([front_row, queries[:lead]], axis=0))
    first_grad = blockify(jnp.concatenate([front_row, out_grad[:lead]], axis=0))
    front_out, front_query, front_keys, front_term = cross_attend(
        first_block,
        first_grad,
        earlier_keys[None],
        earlier_usable[None],
        earlier_present[None],
        gate_tanh,
    )
    local_out, local_query, key_grad, local_term = cross_attend(
        blocks, grad_blocks, keys, usable, present, gate_tanh
    )
    returned = shifted(front_keys[0].astype(jnp.bfloat16), "dp", -1).astype(jnp.float32)
    key_grad = key_grad.at[span_count - 1].add(returned)
    cross_output = jnp.concatenate(
        [front_out.reshape(CH, local_width)[1:], local_out.reshape(row_count, local_width)[:kept]],
        axis=0,
    )
    query_grad = jnp.concatenate(
        [
            front_query.reshape(CH, local_width)[1:],
            local_query.reshape(row_count, local_width)[:kept],
        ],
        axis=0,
    )
    gate_terms = front_term + local_term
    grad_encoded = key_grad.reshape(span_count, NB, NL, head_count, head_dim)
    normed_grad, context_grad = encoder_backward(grad_encoded, normed, saved)
    gain_grad = normed_grad * gains
    projection = lax.psum(jnp.sum(gain_grad * scaled, axis=(3, 4)), "tensor") / full_width
    neighbour_grad = grad_encoded + inverse * (gain_grad - scaled * projection[..., None, None])
    total_tokens = lax.axis_size("group") * lax.axis_size("dp") * row_count
    summed = lax.psum(gate_terms, ("group", "dp"))
    gate_grad = (1.0 - gate_tanh * gate_tanh) * summed / math.sqrt(total_tokens)
    return (
        cross_output,
        query_grad,
        context_grad.reshape(row_count, local_width).astype(jnp.bfloat16),
        neighbour_grad.reshape(-1, local_width).astype(jnp.bfloat16),
        gate_grad,
    )


def solution(mesh):
    return jax.shard_map(
        shards,
        mesh=mesh,
        in_specs=(
            P(("group", "dp"), "tensor"),
            P(("group", "dp"), "tensor"),
            P(("group", "dp"), "tensor"),
            P("group", None),
            P("tensor"),
            P("tensor"),
            P(("group", "dp"), "tensor"),
        ),
        out_specs=(
            P(("group", "dp"), "tensor"),
            P(("group", "dp"), "tensor"),
            P(("group", "dp"), "tensor"),
            P(("group", "dp"), "tensor"),
            P("tensor"),
        ),
        check_vma=False,
    )
```

profile of v0, /device:TPU:1, one launch (start us, length us, event | category | flops | bytes accessed | tf_op | source)
XLA Modules:
  0.0 356.8 jit_solution(13486729681499176493)
XLA Ops:
  0.6 1.5 fusion.4
  2.2 2.8 convert_bitcast_fusion
  5.0 9.3 %psum.21 = f32[2,2,128]{2,1,0:T(2,128)S(1)} all-reduce(f32[2,2,128]{2,1,0:T(2,128)S(1)} %bitcast.184), channel_id=1, replica_groups=mesh['group'=4,'dp'=32,'tensor'=4] {'tensor'}, use_global_device_ids=true, to_apply=%region_1.0 | all-reduce | flops 512 | bytes 4096 | tf_op jit(solution)/shard_map/psum | solution.py:100
  14.4 2.1 copy.109
  18.2 2.4 fusion.6
  22.9 6.3 %collective-permute-start = (bf16[256,8,128]{2,0,1:T(8,128)(2,1)}, bf16[256,8,128]{2,0,1:T(8,128)(2,1)}, u32[]{:S(2)}, u32[]{:S(2)}) collective-permute-start(bf16[256,8,128]{2,0,1:T(8,128)(2,1)} %copy.79), channel_id=1, source_target_pairs={{0,4},{4,8},{8,12},{12,16},{16,20},{20,24},{24,28},{28,32},{32,36}... | collective-permute-start | bytes 1572872 | tf_op jit(solution)/shard_map/ppermute | solution.py:20
  30.4 1.2 iota_compare_fusion.1
  32.4 1.9 copy.82
  39.1 1.2 fusion.66
  40.3 5.0 %multiply_reduce_fusion.1 = (f32[8]{0:T(128)}, f32[2,64,8]{1,2,0:T(8,128)}, bf16[2,64,8,128]{3,1,2,0:T(8,128)(2,1)}) fusion(f32[2,64,8,128]{3,2,1,0:T(8,128)} %bitcast.171, f32[8]{0:T(128)} %tanh.3, pred[2]{0:T(512)(128)(4,1)} %get-tuple-element.21, bf16[2,256,8,128]{3,2,1,0:T(8,128)(2,1)S(1)} %bitcast.155, f32[2,8,64]{2,1,0:T(8,128)S(1)} %get-tuple-element.30, ...), kind=kOutput, calls=%fused_computation.63 | convolution fusion | flops 69075192 | bytes 2891842 | tf_op jit(solution)/shard_map/bhrm,bmhd->brhd/dot_general | solution.py:24
  45.3 2.0 fusion.13
  47.3 1.0 fusion.26
  48.3 1.9 fusion.41
  52.4 6.2 %add_bitcast_fusion.1 = f32[2,256,8,128]{1,3,2,0:T(8,128)} fusion(f32[2,8,128,256]{3,2,1,0:T(8,128)} %fusion.41, f32[2,64,8,128]{3,2,1,0:T(8,128)} %bitcast.173, f32[8]{0:T(128)S(1)} %copy-done.14, pred[2]{0:T(512)(128)(4,1)S(1)} %copy-done.16, f32[2,8,64]{2,1,0:T(8,128)S(1)} %get-tuple-element.30, f32[2,8,64,256]{3,2,1,0:T(8,128)} %copy-done.3), kind=kOutput, calls=%fused_computation.18 | convolution fusion | flops 68814080 | bytes 5771298 | tf_op jit(solution)/shard_map/bhrm,brhd->bmhd/dot_general | solution.py:24
  58.5 1.4 fusion.21
  60.8 2.8 multiply_reduce_fusion.3
  63.6 1.6 fusion.24
  65.2 1.3 fusion.45
  66.6 3.4 fusion.17
  70.0 3.0 collective-permute-start.1
  73.0 1.0 fusion.40
  74.0 252.5 %psum.23 = f32[8]{0:T(128)S(1)} all-reduce(f32[8]{0:T(128)S(1)} %add.79), channel_id=1, replica_groups=mesh['group'=4,'dp'=32,'tensor'=4] {'group','dp'}, use_global_device_ids=true, to_apply=%region_15.16 | all-reduce | flops 8 | bytes 64 | tf_op jit(solution)/shard_map/psum | solution.py:158
  326.7 1.3 fusion.27
  329.6 2.3 fusion.28
  331.9 3.0 copy.96
  334.9 1.9 convert_element_type.156
  337.1 2.3 fusion.7
  339.5 1.2 multiply_convert_fusion
  342.2 2.6 multiply_reduce_fusion
  345.7 6.0 %psum.22 = f32[2,2,128]{2,1,0:T(2,128)S(1)} all-reduce(f32[2,2,128]{2,1,0:T(2,128)S(1)} %get-tuple-element.35), channel_id=1, replica_groups=mesh['group'=4,'dp'=32,'tensor'=4] {'tensor'}, use_global_device_ids=true, to_apply=%region_12.13 | all-reduce | flops 512 | bytes 4096 | tf_op jit(solution)/shard_map/psum | solution.py:155
  351.7 3.1 add_convert_fusion
  355.5 1.3 copy.177
  (104 shorter events, 18.2 us)
Async XLA Ops:
  0.6 13.7 %copy-start.10 = (bf16[128,1024]{1,0:T(8,128)(2,1)S(1)}, bf16[128,1024]{1,0:T(8,128)(2,1)}, u32[]{:S(2)}) copy-start(bf16[128,1024]{1,0:T(8,128)(2,1)} %param.10) | copy-start | bytes 786436
  14.4 2.1 copy-start.13
  17.0 1.0 copy-start.1
  17.2 1.0 copy-start.5
  18.0 2.6 copy-start.21
  18.0 2.6 copy-start.23
  20.6 1.0 copy-start.4
  20.6 8.6 %copy-start.15 = (s32[1,64]{1,0:T(1,128)S(1)}, s32[1,64]{1,0:T(1,128)}, u32[]{:S(2)}) copy-start(s32[1,64]{1,0:T(1,128)} %param.12) | copy-start | bytes 772
  20.6 11.1 %copy-start.9 = (bf16[128,1024]{1,0:T(8,128)(2,1)S(1)}, bf16[128,1024]{1,0:T(8,128)(2,1)}, u32[]{:S(2)}) copy-start(bf16[128,1024]{1,0:T(8,128)(2,1)} %param.9) | copy-start | bytes 786436
  20.6 11.1 %copy-start.8 = (bf16[128,1024]{1,0:T(8,128)(2,1)S(1)}, bf16[128,1024]{1,0:T(8,128)(2,1)}, u32[]{:S(2)}) copy-start(bf16[128,1024]{1,0:T(8,128)(2,1)} %param.15) | copy-start | bytes 786436
  22.0 12.4 %copy-start.17 = (f32[8]{0:T(128)S(1)}, f32[8]{0:T(128)}, u32[]{:S(2)}) copy-start(f32[8]{0:T(128)} %param.14) | copy-start | bytes 100
  22.9 35.6 %collective-permute-start = (bf16[256,8,128]{2,0,1:T(8,128)(2,1)}, bf16[256,8,128]{2,0,1:T(8,128)(2,1)}, u32[]{:S(2)}, u32[]{:S(2)}) collective-permute-start(bf16[256,8,128]{2,0,1:T(8,128)(2,1)} %copy.79), channel_id=1, source_target_pairs={{0,4},{4,8},{8,12},{12,16},{16,20},{20,24},{24,28},{28,32},{32,36}... | collective-permute-start | bytes 1572872 | tf_op jit(solution)/shard_map/ppermute | solution.py:20
  38.1 1.0 copy-start.3
  48.3 1.9 slice-start
  48.3 3.4 copy-start.7
  50.2 1.8 copy-start.12
  50.2 2.1 copy-start.20
  50.2 2.1 copy-start.14
  50.2 2.1 copy-start.16
  58.5 2.3 copy-start.11
  65.2 7.7 %copy-start.19 = (f32[8]{0:T(128)S(1)}, f32[8]{0:T(128)}, u32[]{:S(2)}) copy-start(f32[8]{0:T(128)} %get-tuple-element.17) | copy-start | bytes 100
  70.0 259.6 %collective-permute-start.1 = (bf16[256,8,128]{0,2,1:T(8,128)(2,1)}, bf16[256,8,128]{0,2,1:T(8,128)(2,1)S(1)}, u32[]{:S(2)}, u32[]{:S(2)}) collective-permute-start(bf16[256,8,128]{0,2,1:T(8,128)(2,1)} %fusion.17), channel_id=1, source_target_pairs={{4,0},{8,4},{12,8},{16,12},{20,16},{24,20},{28,24},{32,28},{36,32}... | collective-permute-start | bytes 1572872 | tf_op jit(solution)/shard_map/ppermute | solution.py:20
  73.0 256.1 %copy-start.18 = (f32[8]{0:T(128)S(1)}, f32[8]{0:T(128)}, u32[]{:S(2)}) copy-start(f32[8]{0:T(128)} %param.14) | copy-start | bytes 100
  334.9 2.2 copy-start
  334.9 4.6 %copy-start.22 = (f32[2,2,8,128,192]{3,4,2,1,0:T(8,128)S(1)}, f32[2,2,8,128,192]{3,4,2,1,0:T(8,128)}, u32[]{:S(2)}) copy-start(f32[2,2,8,128,192]{3,4,2,1,0:T(8,128)} %copy-done.21) | copy-start | bytes 9437188
  337.1 2.3 copy-start.2
  337.1 2.4 copy-start.6
  337.1 2.4 copy-start.24
where the time goes:
time: 362 us; the launch traced here: 357 us
  blocking collectives  268 us (74%)
  matrix products  36.8 us (10%)
  other arithmetic  22.9 us (6%)
  local copies, waits for them, and re-layouts  18.3 us (5%)
  starting transfers between devices  9.27 us (3%)
    psum x1, blocking collectives, shards(): summed = lax.psum(gate_terms, ('group', 'dp'))  253 us
    dot_general x18, matrix products, product(): return jnp.einsum(form, left, right, preferred_element_type=jnp.float32)  36.8 us
    ppermute x2, starting transfers between devices, shifted(): lax.ppermute(value, axis, [(source, source + steps) for source in range(l...  9.27 us
    psum x1, blocking collectives, shards(): square_sum = lax.psum(jnp.sum(floats * floats, axis=(3, 4)), 'tensor')  9.27 us
    unnamed x66, local copies, waits for them, and re-layouts  8.57 us
  transfers between devices with their start and end apart: 2, of which 0 were waited for; matrix products, arithmetic and copies ran while one was open for 9% of the time, Pallas kernels for 0%

commit v1 on v0

v1 whole, which is shorter than its diff:
```python
import functools
import math

import jax
import jax.numpy as jnp
from jax import lax
from jax.experimental import pallas as pl
from jax.experimental.pallas import tpu as pltpu
from jax.sharding import PartitionSpec as P

CH = 64
NB = 2
NL = 128
HD = 128
KEYS = NL + CH
EPSILON = 1e-05
MASKED = -1e30
VMEM_LIMIT = 48 * 1024 * 1024

f32 = jnp.float32
bf16 = jnp.bfloat16


def dot(left, right, left_dim, right_dim):
    return lax.dot_general(
        left, right, (((left_dim,), (right_dim,)), ((), ())), preferred_element_type=f32
    )


def cost(flops, nbytes):
    return pl.CostEstimate(flops=flops, bytes_accessed=nbytes, transcendentals=0)


def columns(row):
    return jnp.transpose(jnp.broadcast_to(row, (NL, NL)))


def row_sums(block):
    return jnp.sum(jnp.transpose(block), axis=0, keepdims=True)


def inverse_rows(square_ref, full_width):
    total = (square_ref[0] + square_ref[1]) + (square_ref[2] + square_ref[3])
    return lax.rsqrt(total / full_width + EPSILON)


def squares_kernel(x_ref, q_ref, o_ref, sum_ref, pack_ref):
    step = pl.program_id(0)
    width = x_ref.shape[1]
    total = jnp.zeros((NL, HD), f32)
    for at in range(0, width, HD):
        part = x_ref[:, at : at + HD].astype(f32)
        total = total + part * part
    row = row_sums(total)
    for device in range(sum_ref.shape[0]):
        sum_ref[device, pl.ds(step, 1), :] = row

    @pl.when(step == 0)
    def _():
        pack_ref[0:CH, :] = q_ref[...]
        pack_ref[CH : 2 * CH, :] = o_ref[...]


def squares(x, queries, out_grad, ranks):
    rows, width = x.shape
    count = rows // NL
    half = pl.BlockSpec((CH, width), lambda i: (0, 0))
    return pl.pallas_call(
        squares_kernel,
        grid=(count,),
        in_specs=[pl.BlockSpec((NL, width), lambda i: (i, 0)), half, half],
        out_specs=[
            pl.BlockSpec((ranks, count, NL), lambda i: (0, 0, 0)),
            pl.BlockSpec((2 * CH, width), lambda i: (0, 0)),
        ],
        out_shape=[
            jax.ShapeDtypeStruct((ranks, count, NL), f32),
            jax.ShapeDtypeStruct((2 * CH, width), bf16),
        ],
        cost_estimate=cost(2 * rows * width, 2 * rows * width),
    )(x, queries, out_grad)


def cross(block, grad_block, keys, count, gate_row):
    scale = 1.0 / math.sqrt(HD)
    lane = lax.broadcasted_iota(jnp.int32, (CH, NB * NL), 1)
    scores = dot(block, keys, 1, 1) * scale
    scores = jnp.where(lane < count * NL, scores, MASKED)
    highest = jnp.max(scores, axis=-1, keepdims=True)
    powers = jnp.exp(scores - highest)
    weights = powers * (1.0 / jnp.sum(powers, axis=-1, keepdims=True))
    rounded = weights.astype(bf16)
    present = count > 0
    attended = jnp.where(present, dot(rounded, keys, 1, 0), 0.0)
    output = gate_row * attended
    term = jnp.sum(grad_block * attended, axis=0, keepdims=True)
    att_grad = jnp.where(present, gate_row * grad_block, 0.0)
    att_rounded = att_grad.astype(bf16)
    grad_weights = dot(att_rounded, keys, 1, 1)
    offset = jnp.sum(att_grad * attended, axis=-1, keepdims=True)
    score_grad = (weights * (grad_weights - offset) * scale).astype(bf16)
    query_grad = dot(score_grad, keys, 1, 0)
    key_grad = dot(
        jnp.concatenate([score_grad, rounded], axis=0),
        jnp.concatenate([block, att_rounded], axis=0),
        0,
        0,
    )
    return output, query_grad, key_grad, term


def forward_kernel(
    full_width,
    counts_ref,
    gate_ref,
    square_ref,
    gain_ref,
    x_ref,
    context_ref,
    q_ref,
    o_ref,
    next_q_ref,
    next_o_ref,
    normed_ref,
    prob_ref,
    grad_ref,
    out_ref,
    query_ref,
    back_ref,
    term_ref,
    inverse_ref,
):
    head = pl.program_id(0)
    slots = x_ref.shape[0] // NL
    spans = slots // NB

    @pl.when(head == 0)
    def _():
        inverse = inverse_rows(square_ref, full_width)
        for n in range(slots):
            inverse_ref[n * NL : (n + 1) * NL, :] = columns(inverse[n : n + 1, :])
        term_ref[...] = jnp.zeros_like(term_ref)

    gain = gain_ref[...]
    gate_row = jnp.tanh(jnp.full((1, HD), gate_ref[head], f32))
    encoded = []
    for n in range(slots):
        rows = slice(n * NL, (n + 1) * NL)
        span = n // NB
        x = x_ref[rows, :].astype(f32)
        normed = ((x * inverse_ref[rows, :]) * gain).astype(bf16)
        normed_ref[rows, :] = normed
        keys = jnp.concatenate([normed, context_ref[span * CH : (span + 1) * CH, :]], axis=0)
        powers = jnp.exp(dot(keys, normed, 1, 1) * (1.0 / HD))
        total = jnp.sum(powers, axis=0, keepdims=True)
        rounded = (powers * (1.0 / total)).astype(bf16)
        prob_ref[n] = rounded
        encoded.append((x + dot(rounded, keys, 0, 0)).astype(bf16))

    last = lax.broadcasted_iota(jnp.int32, (CH, HD), 0) == CH - 1

    def blocks(own_ref, next_ref):
        own = own_ref[...].astype(f32)
        following = next_ref[...].astype(f32)
        first = jnp.where(last, own[CH - 1 : CH, :], own[CH:, :])
        second = jnp.where(last, own[2 * CH - 1 :, :], following)
        return first, second

    q_blocks = blocks(q_ref, next_q_ref)
    o_blocks = blocks(o_ref, next_o_ref)
    outs, queries, terms = [], [], []
    for span in range(spans):
        keys = jnp.concatenate(encoded[span * NB : (span + 1) * NB], axis=0)
        output, query_grad, key_grad, term = cross(
            q_blocks[span].astype(bf16), o_blocks[span], keys, counts_ref[span], gate_row
        )
        grad_ref[span * NB * NL : (span + 1) * NB * NL, :] = key_grad
        outs.append(output)
        queries.append(query_grad)
        terms.append(term)
    for at, (target, pair) in enumerate(((out_ref, outs), (query_ref, queries))):
        first, second = pair
        target[0:CH, :] = jnp.broadcast_to(first[CH - 1 :, :], (CH, HD)).astype(bf16)
        target[CH:, :] = jnp.where(last, second[CH - 1 :, :], first).astype(bf16)
        back_ref[at * CH : (at + 1) * CH, :] = second.astype(bf16)
    lane = lax.broadcasted_iota(jnp.int32, (1, HD), 1)
    value = jnp.sum(terms[0] + terms[1], axis=-1, keepdims=True)
    term_ref[...] += jnp.where(lane == head, value, 0.0)


def forward(own_counts, head_gate, squares_all, gain, x, context, queries, out_grad, arrived, full_width):
    rows, width = x.shape
    heads = width // HD
    tokens = queries.shape[0]
    slots = rows // NL

    def tall(size):
        return pl.BlockSpec((size, HD), lambda h: (0, h))

    smem = pl.BlockSpec(memory_space=pltpu.SMEM)
    return pl.pallas_call(
        functools.partial(forward_kernel, full_width),
        grid=(heads,),
        in_specs=[
            smem,
            smem,
            pl.BlockSpec(squares_all.shape, lambda h: (0, 0, 0)),
            pl.BlockSpec((1, HD), lambda h: (0, h)),
            tall(rows),
            tall(tokens),
            tall(tokens),
            tall(tokens),
            tall(CH),
            pl.BlockSpec((CH, HD), lambda h: (1, h)),
        ],
        out_specs=[
            tall(rows),
            pl.BlockSpec((None, slots, KEYS, NL), lambda h: (h, 0, 0, 0)),
            tall(rows),
            tall(tokens),
            tall(tokens),
            tall(tokens),
            pl.BlockSpec((1, HD), lambda h: (0, 0)),
        ],
        out_shape=[
            jax.ShapeDtypeStruct((rows, width), bf16),
            jax.ShapeDtypeStruct((heads, slots, KEYS, NL), bf16),
            jax.ShapeDtypeStruct((rows, width), f32),
            jax.ShapeDtypeStruct((tokens, width), bf16),
            jax.ShapeDtypeStruct((tokens, width), bf16),
            jax.ShapeDtypeStruct((tokens, width), bf16),
            jax.ShapeDtypeStruct((1, HD), f32),
        ],
        scratch_shapes=[pltpu.VMEM((rows, HD), f32)],
        compiler_params=pltpu.CompilerParams(vmem_limit_bytes=VMEM_LIMIT),
        cost_estimate=cost(4 * 10**9, 10**7),
    )(own_counts, head_gate, squares_all, gain, x, context, queries, out_grad, arrived, arrived)


def backward_kernel(
    full_width,
    square_ref,
    gain_ref,
    x_ref,
    context_ref,
    normed_ref,
    prob_ref,
    grad_ref,
    mid_ref,
    context_grad_ref,
    project_ref,
    inverse_ref,
    total_ref,
):
    head = pl.program_id(0)
    slots = x_ref.shape[0] // NL

    @pl.when(head == 0)
    def _():
        inverse = inverse_rows(square_ref, full_width)
        for n in range(slots):
            inverse_ref[n * NL : (n + 1) * NL, :] = columns(inverse[n : n + 1, :])
        total_ref[...] = jnp.zeros_like(total_ref)

    gain = gain_ref[...]
    context_sum = None
    for n in range(slots):
        rows = slice(n * NL, (n + 1) * NL)
        span = n // NB
        normed = normed_ref[rows, :]
        keys = jnp.concatenate([normed, context_ref[span * CH : (span + 1) * CH, :]], axis=0)
        grad = grad_ref[rows, :]
        grad_rounded = grad.astype(bf16)
        prob = prob_ref[n]
        weights = prob.astype(f32)
        grad_weights = dot(keys, grad_rounded, 1, 1)
        offset = jnp.sum(weights * grad_weights, axis=0, keepdims=True)
        score_grad = (weights * (grad_weights - offset) * (1.0 / HD)).astype(bf16)
        key_grad = dot(
            jnp.concatenate([score_grad, prob], axis=1),
            jnp.concatenate([normed, grad_rounded], axis=0),
            1,
            0,
        )
        normed_grad = dot(score_grad, keys, 0, 0) + key_grad[:NL, :]
        gained = normed_grad * gain
        inverse = inverse_ref[rows, :]
        scaled = x_ref[rows, :].astype(f32) * inverse
        total_ref[rows, :] += gained * scaled
        mid_ref[rows, :] = grad + inverse * gained
        part = key_grad[NL:, :]
        if n % NB == 0:
            context_sum = part
        else:
            context_grad_ref[span * CH : (span + 1) * CH, :] = (context_sum + part).astype(bf16)

    @pl.when(head == pl.num_programs(0) - 1)
    def _():
        for n in range(slots):
            row = row_sums(total_ref[n * NL : (n + 1) * NL, :])
            for device in range(project_ref.shape[0]):
                project_ref[device, n : n + 1, :] = row


def backward(squares_all, gain, x, context, normed, prob, grad, full_width):
    rows, width = x.shape
    heads = width // HD
    tokens = context.shape[0]
    slots = rows // NL

    def tall(size):
        return pl.BlockSpec((size, HD), lambda h: (0, h))

    whole = pl.BlockSpec(squares_all.shape, lambda h: (0, 0, 0))
    return pl.pallas_call(
        functools.partial(backward_kernel, full_width),
        grid=(heads,),
        in_specs=[
            whole,
            pl.BlockSpec((1, HD), lambda h: (0, h)),
            tall(rows),
            tall(tokens),
            tall(rows),
            pl.BlockSpec((None, slots, KEYS, NL), lambda h: (h, 0, 0, 0)),
            tall(rows),
        ],
        out_specs=[tall(rows), tall(tokens), whole],
        out_shape=[
            jax.ShapeDtypeStruct((rows, width), f32),
            jax.ShapeDtypeStruct((tokens, width), bf16),
            jax.ShapeDtypeStruct(squares_all.shape, f32),
        ],
        scratch_shapes=[pltpu.VMEM((rows, HD), f32), pltpu.VMEM((rows, HD), f32)],
        compiler_params=pltpu.CompilerParams(vmem_limit_bytes=VMEM_LIMIT),
        cost_estimate=cost(4 * 10**9, 10**7),
    )(squares_all, gain, x, context, normed, prob, grad)


def final_kernel(
    full_width,
    square_ref,
    project_ref,
    x_ref,
    mid_ref,
    out_in_ref,
    query_in_ref,
    ret_out_ref,
    ret_query_ref,
    grad_ref,
    out_ref,
    query_ref,
    factor_ref,
):
    step = pl.program_id(0)
    slots = x_ref.shape[0] // NL

    @pl.when(step == 0)
    def _():
        inverse = inverse_rows(square_ref, full_width)
        project = (project_ref[0] + project_ref[1]) + (project_ref[2] + project_ref[3])
        factor = inverse * inverse * (project / full_width)
        for n in range(slots):
            factor_ref[n * NL : (n + 1) * NL, :] = columns(factor[n : n + 1, :])

    width = x_ref.shape[1]
    factor = factor_ref[...]
    for at in range(0, width, HD):
        cols = slice(at, at + HD)
        x = x_ref[:, cols].astype(f32)
        grad_ref[:, cols] = (mid_ref[:, cols] - x * factor).astype(bf16)
    last = lax.broadcasted_iota(jnp.int32, (CH, width), 0) == CH - 1
    for own, back, target in (
        (out_in_ref, ret_out_ref, out_ref),
        (query_in_ref, ret_query_ref, query_ref),
    ):
        own_rows = own[...].astype(f32)
        target[...] = jnp.where(last, own_rows, back[...].astype(f32)).astype(bf16)


def final(squares_all, projects_all, x, mid, out, query, returned, full_width):
    rows, width = x.shape
    tokens = out.shape[0]
    part = 2 * HD
    whole = pl.BlockSpec(squares_all.shape, lambda i: (0, 0, 0))
    tall = pl.BlockSpec((rows, part), lambda i: (0, i))
    half = pl.BlockSpec((CH, part), lambda i: (0, i))
    return pl.pallas_call(
        functools.partial(final_kernel, full_width),
        grid=(width // part,),
        in_specs=[
            whole,
            whole,
            tall,
            tall,
            half,
            half,
            half,
            pl.BlockSpec((CH, part), lambda i: (1, i)),
        ],
        out_specs=[tall, half, half],
        out_shape=[
            jax.ShapeDtypeStruct((rows, width), bf16),
            jax.ShapeDtypeStruct((tokens, width), bf16),
            jax.ShapeDtypeStruct((tokens, width), bf16),
        ],
        scratch_shapes=[pltpu.VMEM((rows, HD), f32)],
        input_output_aliases={4: 1, 5: 2},
        compiler_params=pltpu.CompilerParams(vmem_limit_bytes=VMEM_LIMIT),
        cost_estimate=cost(4 * rows * width, 8 * rows * width),
    )(squares_all, projects_all, x, mid, out, query, returned, returned)


def shards(queries, span_state, neigh_state, counts, norm_gain, head_gate, out_grad):
    head_count = head_gate.shape[0]
    width = queries.shape[1]
    row_count = queries.shape[0]
    span_count = row_count // CH
    ranks = lax.axis_size("tensor")
    full_width = float(ranks * width)
    lines = lax.axis_size("dp")

    local_squares, pack = squares(neigh_state, queries, out_grad, ranks)
    arrived = lax.ppermute(pack, "dp", [(i, i - 1) for i in range(1, lines)])
    squares_all = lax.all_to_all(local_squares, "tensor", 0, 0, tiled=True)
    gain = norm_gain[None, :]
    first_span = lax.axis_index("dp") * span_count
    own_counts = lax.dynamic_slice_in_dim(counts.reshape(-1), first_span, span_count)
    normed, prob, grad, out, query, back, term = forward(
        own_counts, head_gate, squares_all, gain, neigh_state, span_state, queries, out_grad,
        arrived, full_width,
    )
    gathered = lax.all_to_all(jnp.broadcast_to(term, (lines, HD)), "dp", 0, 0, tiled=True)
    summed = jnp.sum(gathered, axis=0)
    returned = lax.ppermute(back, "dp", [(i, i + 1) for i in range(lines - 1)])
    mid, context_grad, local_project = backward(
        squares_all, gain, neigh_state, span_state, normed, prob, grad, full_width
    )
    projects_all = lax.all_to_all(local_project, "tensor", 0, 0, tiled=True)
    for step in (1, 2):
        count = lax.axis_size("group")
        summed = summed + lax.ppermute(summed, "group", [(i, i ^ step) for i in range(count)])
    neighbour_grad, out, query = final(
        squares_all, projects_all, neigh_state, mid, out, query, returned, full_width
    )
    gate_tanh = jnp.tanh(head_gate)
    total_tokens = lax.axis_size("group") * lines * row_count
    gate_grad = (1.0 - gate_tanh * gate_tanh) * summed[:head_count] / math.sqrt(total_tokens)
    return out, query, context_grad, neighbour_grad, gate_grad


def solution(mesh):
    rows = P(("group", "dp"), "tensor")
    return jax.shard_map(
        shards,
        mesh=mesh,
        in_specs=(rows, rows, rows, P("group", None), P("tensor"), P("tensor"), rows),
        out_specs=(rows, rows, rows, rows, P("tensor")),
        check_vma=False,
    )
```

time: 362 us -> 109 us (0.30)
  blocking collectives: 268 us -> 12.4 us
  Pallas kernels: 0 us -> 37.9 us
  matrix products: 36.8 us -> 0 us
  starting transfers between devices: 9.27 us -> 36.6 us
  other arithmetic: 22.9 us -> 0.55 us
  waiting for transfers between devices: 0.01 us -> 7.77 us
  local copies, waits for them, and re-layouts: 18.3 us -> 11.2 us
    psum x3 -> x0, blocking collectives: 268 us -> none  [the longest x1 253 us: shards(): summed = lax.psum(gate_terms, ('group', 'dp'))]
    pallas_call x0 -> x4, Pallas kernels: none -> 37.9 us  [the longest x1 19.5 us: forward(): pl.pallas_call(functools.partial(forward_kernel, full_width), grid=(heads...]
    dot_general x18 -> x0, matrix products: 36.8 us -> none  [product(): return jnp.einsum(form, left, right, preferred_element_type=jnp.float32)]
    ppermute x2 -> x4, starting transfers between devices: 9.27 us -> 30.1 us  [the longest x2 18.2 us: shards(): lax.ppermute(summed, 'group', [(i, i ^ step) for i in range(count)])]
    all_to_all x0 -> x1, blocking collectives: none -> 12.4 us  [shards(): lax.all_to_all(jnp.broadcast_to(term, (lines, HD)), 'dp', 0, 0, tiled=True)]
    all_to_all x0 -> x2, waiting for transfers between devices: none -> 7.76 us  [the longest x1 4.18 us: shards(): squares_all = lax.all_to_all(local_squares, 'tensor', 0, 0, tiled=True)]
    convert_element_type x4 -> x0, other arithmetic: 6.59 us -> none  [the longest x1 3.13 us: shards(): neighbour_grad.reshape(-1, local_width).astype(jnp.bfloat16)]
    all_to_all x0 -> x2, starting transfers between devices: none -> 6.51 us  [the longest x1 3.26 us: shards(): squares_all = lax.all_to_all(local_squares, 'tensor', 0, 0, tiled=True)]
  transfers between devices with their start and end apart: 2 -> 6, of which waited for: 0 -> 2; matrix products, arithmetic and copies ran while one was open for 9% -> 1% of each run, Pallas kernels for 0% -> 11%
where the time goes in v1:
time: 109 us; the launch traced here: 107 us
  Pallas kernels  37.9 us (35%)
  starting transfers between devices  36.6 us (34%)
  blocking collectives  12.4 us (11%)
  local copies, waits for them, and re-layouts  11.2 us (10%)
  waiting for transfers between devices  7.77 us (7%)
    pallas_call x1, Pallas kernels, forward(): pl.pallas_call(functools.partial(forward_kernel, full_width), grid=(heads...  19.5 us
    ppermute x2, starting transfers between devices, shards(): lax.ppermute(summed, 'group', [(i, i ^ step) for i in range(count)])  18.2 us
    all_to_all x1, blocking collectives, shards(): lax.all_to_all(jnp.broadcast_to(term, (lines, HD)), 'dp', 0, 0, tiled=True)  12.4 us
    pallas_call x1, Pallas kernels, backward(): pl.pallas_call(functools.partial(backward_kernel, full_width), grid=(head...  11.8 us
    unnamed x30, local copies, waits for them, and re-layouts  11.1 us
    ppermute x1, starting transfers between devices, shards(): arrived = lax.ppermute(pack, 'dp', [(i, i - 1) for i in range(1, lines)])  8.77 us
    all_to_all x1, waiting for transfers between devices, shards(): squares_all = lax.all_to_all(local_squares, 'tensor', 0, 0, tiled=True)  4.18 us
    all_to_all x1, waiting for transfers between devices, shards(): projects_all = lax.all_to_all(local_project, 'tensor', 0, 0, tiled=True)  3.58 us
  transfers between devices with their start and end apart: 6, of which 2 were waited for; matrix products, arithmetic and copies ran while one was open for 1% of the time, Pallas kernels for 11%

profile of v1, /device:TPU:1, one launch (start us, length us, event | category | flops | bytes accessed | tf_op | source)
XLA Modules:
  0.0 107.2 jit_solution(988484815483918534)
XLA Ops:
  0.6 0.0 copy-start
  0.6 3.2 %shard_map.110 = (f32[4,4,128]{2,1,0:T(4,128)}, bf16[128,1024]{1,0:T(8,128)(2,1)}) custom-call(bf16[512,1024]{1,0:T(8,128)(2,1)} %x_ref.7, bf16[128,1024]{1,0:T(8,128)(2,1)} %q_ref.3, bf16[128,1024]{1,0:T(8,128)(2,1)} %o_ref.3), custom_call_target="tpu_custom_call" | custom-call | flops 1048576 | bytes 1048576 | tf_op jit(solution)/shard_map/pallas_call | solution.py:68
  3.8 8.8 %collective-permute-start = (bf16[128,1024]{1,0:T(8,128)(2,1)}, bf16[128,1024]{1,0:T(8,128)(2,1)S(1)}, u32[]{:S(2)}, u32[]{:S(2)}) collective-permute-start(bf16[128,1024]{1,0:T(8,128)(2,1)} %get-tuple-element.21), channel_id=1, source_target_pairs={{4,0},{8,4},{12,8},{16,12},{20,16},{24,20},{28,24},{32,28},{36,32}... | collective-permute-start | bytes 786440 | tf_op jit(solution)/shard_map/ppermute | solution.py:423
  12.6 3.3 %all-to-all-start = ((f32[4,4,128]{2,1,0:T(4,128)}), f32[4,4,128]{2,1,0:T(4,128)S(1)}, u32[]{:S(2)}, u32[]{:S(2)}) async-start(f32[4,4,128]{2,1,0:T(4,128)} %get-tuple-element.20), calls=%async_computation | async-start | bytes 16384 | tf_op jit(solution)/shard_map/all_to_all | solution.py:424
  15.9 0.1 dynamic-slice_bitcast_fusion.counts_ref
  15.9 4.2 %all-to-all-done.square_ref = f32[4,4,128]{2,1,0:T(4,128)S(1)} async-done(((f32[4,4,128]{2,1,0:T(4,128)}), f32[4,4,128]{2,1,0:T(4,128)S(1)}, u32[]{:S(2)}, u32[]{:S(2)}) %all-to-all-start) | async-done | bytes 8224 | tf_op jit(solution)/shard_map/all_to_all | solution.py:424
  20.1 0.0 collective-permute-done.next_q_ref.next_o_ref
  20.1 1.2 %copy-done.1 = bf16[512,1024]{1,0:T(8,128)(2,1)S(1)} copy-done((bf16[512,1024]{1,0:T(8,128)(2,1)S(1)}, bf16[512,1024]{1,0:T(8,128)(2,1)}, u32[]{:S(2)}) %copy-start.1) | copy-done | bytes 1048600
  21.4 0.9 copy-done.3
  22.3 0.9 copy-done.4
  23.3 0.9 copy-done.5
  24.2 0.7 copy-done.7
  24.9 0.7 copy-done.9
  25.6 19.5 %shard_map.111 = (bf16[512,1024]{1,0:T(8,128)(2,1)S(1)}, bf16[8,4,192,128]{3,2,1,0:T(8,128)(2,1)S(1)}, f32[512,1024]{1,0:T(8,128)}, bf16[128,1024]{1,0:T(8,128)(...) custom-call(s32[2]{0:T(128)S(1)} %dynamic-slice_bitcast_fusion.counts_ref, ...), custom_call_target="tpu_custom_call" | custom-call | flops 4000000000 | bytes 10000000 | tf_op jit(solution)/shard_map/pallas_call | solution.py:201
  45.1 1.1 %copy-done.11 = bf16[8,4,192,128]{3,2,1,0:T(8,128)(2,1)} copy-done((bf16[8,4,192,128]{3,2,1,0:T(8,128)(2,1)}, bf16[8,4,192,128]{3,2,1,0:T(8,128)(2,1)S(1)}, u32[]{:S(2)}) %copy-start.11) | copy-done | bytes 1572888
  46.2 1.0 copy-done.13
  47.2 12.4 %all_to_all.16 = f32[32,1,128]{2,1,0:T(1,128)S(1)} all-to-all(f32[32,1,128]{2,1,0:T(1,128)S(1)} %broadcast_in_dim.9), channel_id=1, replica_groups=mesh['group'=4,'dp'=32,'tensor'=4] {'dp'}, dimensions={0} | all-to-all | bytes 32768 | tf_op jit(solution)/shard_map/all_to_all | solution.py:432
  59.6 8.8 %collective-permute-start.2 = (f32[128]{0:T(128)S(1)}, f32[128]{0:T(128)S(1)}, u32[]{:S(2)}, u32[]{:S(2)}) collective-permute-start(f32[128]{0:T(128)S(1)} %reduce_sum.9), channel_id=1, source_target_pairs={{0,128},{128,0},{256,384},{384,256},{1,129},{129,1},{257,385},{385... | collective-permute-start | bytes 1544 | tf_op jit(solution)/shard_map/ppermute | solution.py:441
  68.4 3.1 %collective-permute-start.1 = (bf16[128,1024]{1,0:T(8,128)(2,1)}, bf16[128,1024]{1,0:T(8,128)(2,1)S(1)}, u32[]{:S(2)}, u32[]{:S(2)}) collective-permute-start(bf16[128,1024]{1,0:T(8,128)(2,1)} %get-tuple-element.29), channel_id=1, source_target_pairs={{0,4},{4,8},{8,12},{12,16},{16,20},{20,24},{24,28},{28,32},{32,36}... | collective-permute-start | bytes 786440 | tf_op jit(solution)/shard_map/ppermute | solution.py:434
  71.5 0.0 collective-permute-done.2
  71.6 9.4 %collective-permute-start.3 = (f32[128]{0:T(128)S(1)}, f32[128]{0:T(128)S(1)}, u32[]{:S(2)}, u32[]{:S(2)}) collective-permute-start(f32[128]{0:T(128)S(1)} %add.10), channel_id=1, source_target_pairs={{0,256},{128,384},{256,0},{384,128},{1,257},{129,385},{257,1},{385... | collective-permute-start | bytes 1544 | tf_op jit(solution)/shard_map/ppermute | solution.py:441
  81.0 0.0 copy-start.6
  81.0 0.9 copy-done.6
  82.0 1.4 %copy-done.12 = bf16[8,4,192,128]{3,2,1,0:T(8,128)(2,1)S(1)} copy-done((bf16[8,4,192,128]{3,2,1,0:T(8,128)(2,1)S(1)}, bf16[8,4,192,128]{3,2,1,0:T(8,128)(2,1)}, u32[]{:S(2)}) %copy-start.12) | copy-done | bytes 1572888
  83.4 1.2 %copy-done.14 = bf16[512,1024]{1,0:T(8,128)(2,1)S(1)} copy-done((bf16[512,1024]{1,0:T(8,128)(2,1)S(1)}, bf16[512,1024]{1,0:T(8,128)(2,1)}, u32[]{:S(2)}) %copy-start.14) | copy-done | bytes 1048600
  84.6 11.8 %shard_map.112 = (f32[512,1024]{1,0:T(8,128)S(1)}, bf16[128,1024]{1,0:T(8,128)(2,1)}, f32[4,4,128]{2,1,0:T(4,128)}) custom-call(f32[4,4,128]{2,1,0:T(4,128)S(1)} %all-to-all-done.square_ref, f32[1,1024]{1,0:T(1,128)S(1)} %bitcast.7, bf16[512,1024]{1,0:T(8,128)(2,1)S(1)} %copy-done.2, bf16[128,1024]{1,0:T(8,128)(2,1)S(1)} %copy-done.6, ...), custom_call_target="tpu_custom_call" | custom-call | flops 4000000000 | bytes 10000000 | tf_op jit(solution)/shard_map/pallas_call | solution.py:315
  96.4 3.2 %all-to-all-start.1 = ((f32[4,4,128]{2,1,0:T(4,128)}), f32[4,4,128]{2,1,0:T(4,128)S(1)}, u32[]{:S(2)}, u32[]{:S(2)}) async-start(f32[4,4,128]{2,1,0:T(4,128)} %get-tuple-element.25), calls=%async_computation.1 | async-start | bytes 16384 | tf_op jit(solution)/shard_map/all_to_all | solution.py:438
  99.6 0.0 collective-permute-done.3
  99.7 0.5 multiply_multiply_fusion
  100.2 3.6 %all-to-all-done.1.project_ref = f32[4,4,128]{2,1,0:T(4,128)S(1)} async-done(((f32[4,4,128]{2,1,0:T(4,128)}), f32[4,4,128]{2,1,0:T(4,128)S(1)}, u32[]{:S(2)}, u32[]{:S(2)}) %all-to-all-start.1) | async-done | bytes 8224 | tf_op jit(solution)/shard_map/all_to_all | solution.py:438
  103.8 0.0 collective-permute-done.1.ret_out_ref.ret_query_ref
  103.8 3.4 %shard_map.113 = (bf16[512,1024]{1,0:T(8,128)(2,1)}, bf16[128,1024]{1,0:T(8,128)(2,1)}, bf16[128,1024]{1,0:T(8,128)(2,1)}) custom-call(f32[4,4,128]{2,1,0:T(4,128)S(1)} %all-to-all-done.square_ref, f32[4,4,128]{2,1,0:T(4,128)S(1)} %all-to-all-done.1.project_ref, bf16[512,1024]{1,0:T(8,128)(2,1)S(1)} %copy-done.2, ...), custom_call_target="tpu_custom_call", output_to_operand_aliasing={{1}: (4, {}), {2}: (5, {})} | custom-call | flops 2097152 | bytes 4194304 | tf_op jit(solution)/shard_map/pallas_call | solution.py:387
  (21 shorter events, 0.1 us)
Async XLA Ops:
  0.6 15.2 %copy-start = (s32[1,64]{1,0:T(1,128)S(1)}, s32[1,64]{1,0:T(1,128)}, u32[]{:S(2)}) copy-start(s32[1,64]{1,0:T(1,128)} %param.10) | copy-start | bytes 772
  3.8 16.3 %collective-permute-start = (bf16[128,1024]{1,0:T(8,128)(2,1)}, bf16[128,1024]{1,0:T(8,128)(2,1)S(1)}, u32[]{:S(2)}, u32[]{:S(2)}) collective-permute-start(bf16[128,1024]{1,0:T(8,128)(2,1)} %get-tuple-element.21), channel_id=1, source_target_pairs={{4,0},{8,4},{12,8},{16,12},{20,16},{24,20},{28,24},{32,28},{36,32}... | collective-permute-start | bytes 786440 | tf_op jit(solution)/shard_map/ppermute | solution.py:423
  12.6 7.5 %all-to-all-start = ((f32[4,4,128]{2,1,0:T(4,128)}), f32[4,4,128]{2,1,0:T(4,128)S(1)}, u32[]{:S(2)}, u32[]{:S(2)}) async-start(f32[4,4,128]{2,1,0:T(4,128)} %get-tuple-element.20), calls=%async_computation | async-start | bytes 16384 | tf_op jit(solution)/shard_map/all_to_all | solution.py:424
  20.1 1.2 %copy-start.1 = (bf16[512,1024]{1,0:T(8,128)(2,1)S(1)}, bf16[512,1024]{1,0:T(8,128)(2,1)}, u32[]{:S(2)}) copy-start(bf16[512,1024]{1,0:T(8,128)(2,1)} %x_ref.7) | copy-start | bytes 3145732
  21.4 0.9 copy-start.3
  22.3 0.9 copy-start.4
  23.3 0.9 copy-start.5
  24.2 0.7 copy-start.7
  24.9 0.7 copy-start.9
  25.5 55.4 %copy-start.2 = (bf16[512,1024]{1,0:T(8,128)(2,1)S(1)}, bf16[512,1024]{1,0:T(8,128)(2,1)}, u32[]{:S(2)}) copy-start(bf16[512,1024]{1,0:T(8,128)(2,1)} %x_ref.7) | copy-start | bytes 3145732
  25.6 55.4 %copy-start.8 = (f32[1024]{0:T(1024)S(1)}, f32[1024]{0:T(1024)}, u32[]{:S(2)}) copy-start(f32[1024]{0:T(1024)} %param.11) | copy-start | bytes 12292
  45.1 1.1 %copy-start.11 = (bf16[8,4,192,128]{3,2,1,0:T(8,128)(2,1)}, bf16[8,4,192,128]{3,2,1,0:T(8,128)(2,1)S(1)}, u32[]{:S(2)}) copy-start(bf16[8,4,192,128]{3,2,1,0:T(8,128)(2,1)S(1)} %get-tuple-element.23.prob_ref) | copy-start | bytes 4718596
  46.2 1.0 copy-start.13
  59.6 11.9 %collective-permute-start.2 = (f32[128]{0:T(128)S(1)}, f32[128]{0:T(128)S(1)}, u32[]{:S(2)}, u32[]{:S(2)}) collective-permute-start(f32[128]{0:T(128)S(1)} %reduce_sum.9), channel_id=1, source_target_pairs={{0,128},{128,0},{256,384},{384,256},{1,129},{129,1},{257,385},{385... | collective-permute-start | bytes 1544 | tf_op jit(solution)/shard_map/ppermute | solution.py:441
  68.4 35.3 %collective-permute-start.1 = (bf16[128,1024]{1,0:T(8,128)(2,1)}, bf16[128,1024]{1,0:T(8,128)(2,1)S(1)}, u32[]{:S(2)}, u32[]{:S(2)}) collective-permute-start(bf16[128,1024]{1,0:T(8,128)(2,1)} %get-tuple-element.29), channel_id=1, source_target_pairs={{0,4},{4,8},{8,12},{12,16},{16,20},{20,24},{24,28},{28,32},{32,36}... | collective-permute-start | bytes 786440 | tf_op jit(solution)/shard_map/ppermute | solution.py:434
  71.6 28.1 %collective-permute-start.3 = (f32[128]{0:T(128)S(1)}, f32[128]{0:T(128)S(1)}, u32[]{:S(2)}, u32[]{:S(2)}) collective-permute-start(f32[128]{0:T(128)S(1)} %add.10), channel_id=1, source_target_pairs={{0,256},{128,384},{256,0},{384,128},{1,257},{129,385},{257,1},{385... | collective-permute-start | bytes 1544 | tf_op jit(solution)/shard_map/ppermute | solution.py:441
  81.0 1.0 copy-start.6
  82.0 1.4 %copy-start.12 = (bf16[8,4,192,128]{3,2,1,0:T(8,128)(2,1)S(1)}, bf16[8,4,192,128]{3,2,1,0:T(8,128)(2,1)}, u32[]{:S(2)}) copy-start(bf16[8,4,192,128]{3,2,1,0:T(8,128)(2,1)} %copy-done.11) | copy-start | bytes 4718596
  83.4 1.2 %copy-start.14 = (bf16[512,1024]{1,0:T(8,128)(2,1)S(1)}, bf16[512,1024]{1,0:T(8,128)(2,1)}, u32[]{:S(2)}) copy-start(bf16[512,1024]{1,0:T(8,128)(2,1)} %copy-done.13) | copy-start | bytes 3145732
  84.6 15.1 %copy-start.10 = (f32[8]{0:T(128)S(1)}, f32[8]{0:T(128)}, u32[]{:S(2)}) copy-start(f32[8]{0:T(128)} %gate_ref.1) | copy-start | bytes 100
  96.4 7.4 %all-to-all-start.1 = ((f32[4,4,128]{2,1,0:T(4,128)}), f32[4,4,128]{2,1,0:T(4,128)S(1)}, u32[]{:S(2)}, u32[]{:S(2)}) async-start(f32[4,4,128]{2,1,0:T(4,128)} %get-tuple-element.25), calls=%async_computation.1 | async-start | bytes 16384 | tf_op jit(solution)/shard_map/all_to_all | solution.py:438

commit v2 on v1

v2 whole, which is shorter than its diff:
```python
import functools
import math

import jax
import jax.numpy as jnp
from jax import lax
from jax.experimental import pallas as pl
from jax.experimental.pallas import tpu as pltpu
from jax.sharding import PartitionSpec as P

CH = 64
NB = 2
NL = 128
HD = 128
KEYS = NL + CH
EPSILON = 1e-05
MASKED = -1e30
VMEM_LIMIT = 61 * 1024 * 1024
HEADS_PER_STEP = 4
SIDE_BY_SIDE = 4

f32 = jnp.float32
bf16 = jnp.bfloat16


def dot(left, right, left_dim, right_dim):
    return lax.dot_general(
        left, right, (((left_dim,), (right_dim,)), ((), ())), preferred_element_type=f32
    )


def cost(flops, nbytes):
    return pl.CostEstimate(flops=flops, bytes_accessed=nbytes, transcendentals=0)


def columns(row):
    return jnp.transpose(jnp.broadcast_to(row, (NL, NL)))


def row_sums(block):
    return jnp.sum(jnp.transpose(block), axis=0, keepdims=True)


def inverse_rows(square_ref, full_width):
    total = (square_ref[0] + square_ref[1]) + (square_ref[2] + square_ref[3])
    return lax.rsqrt(total / full_width + EPSILON)


def squares_kernel(x_ref, q_ref, o_ref, sum_ref, pack_ref):
    step = pl.program_id(0)
    width = x_ref.shape[1]
    total = jnp.zeros((NL, HD), f32)
    for at in range(0, width, HD):
        part = x_ref[:, at : at + HD].astype(f32)
        total = total + part * part
    row = row_sums(total)
    for device in range(sum_ref.shape[0]):
        sum_ref[device, pl.ds(step, 1), :] = row

    @pl.when(step == 0)
    def _():
        pack_ref[0:CH, :] = q_ref[...]
        pack_ref[CH : 2 * CH, :] = o_ref[...]


def squares(x, queries, out_grad, ranks):
    rows, width = x.shape
    count = rows // NL
    half = pl.BlockSpec((CH, width), lambda i: (0, 0))
    return pl.pallas_call(
        squares_kernel,
        grid=(count,),
        in_specs=[pl.BlockSpec((NL, width), lambda i: (i, 0)), half, half],
        out_specs=[
            pl.BlockSpec((ranks, count, NL), lambda i: (0, 0, 0)),
            pl.BlockSpec((2 * CH, width), lambda i: (0, 0)),
        ],
        out_shape=[
            jax.ShapeDtypeStruct((ranks, count, NL), f32),
            jax.ShapeDtypeStruct((2 * CH, width), bf16),
        ],
        cost_estimate=cost(2 * rows * width, 2 * rows * width),
    )(x, queries, out_grad)


def cross(items):
    scale = 1.0 / math.sqrt(HD)
    lane = lax.broadcasted_iota(jnp.int32, (CH, NB * NL), 1)
    scores = [dot(block, keys, 1, 1) * scale for block, _, keys, _, _ in items]
    scores = [jnp.where(lane < it[3] * NL, sc, MASKED) for it, sc in zip(items, scores)]
    highest = [jnp.max(sc, axis=-1, keepdims=True) for sc in scores]
    powers = [jnp.exp(sc - hi) for sc, hi in zip(scores, highest)]
    sums = [jnp.sum(po, axis=-1, keepdims=True) for po in powers]
    weights = [po * (1.0 / su) for po, su in zip(powers, sums)]
    rounded = [we.astype(bf16) for we in weights]
    attended = [dot(ro, it[2], 1, 0) for it, ro in zip(items, rounded)]
    attended = [jnp.where(it[3] > 0, at, 0.0) for it, at in zip(items, attended)]
    att_grad = [jnp.where(it[3] > 0, it[4] * it[1], 0.0) for it in items]
    att_rounded = [ag.astype(bf16) for ag in att_grad]
    grad_weights = [dot(ar, it[2], 1, 1) for it, ar in zip(items, att_rounded)]
    offset = [jnp.sum(ag * at, axis=-1, keepdims=True) for ag, at in zip(att_grad, attended)]
    score_grad = [
        (we * (gw - of) * scale).astype(bf16) for we, gw, of in zip(weights, grad_weights, offset)
    ]
    query_grad = [dot(sg, it[2], 1, 0) for it, sg in zip(items, score_grad)]
    key_grad = [
        dot(
            jnp.concatenate([sg, ro], axis=0),
            jnp.concatenate([it[0], ar], axis=0),
            0,
            0,
        )
        for it, sg, ro, ar in zip(items, score_grad, rounded, att_rounded)
    ]
    outputs = [it[4] * at for it, at in zip(items, attended)]
    terms = [jnp.sum(it[1] * at, axis=0, keepdims=True) for it, at in zip(items, attended)]
    return outputs, query_grad, key_grad, terms


def main_kernel(
    full_width,
    counts_ref,
    gate_ref,
    square_ref,
    gain_ref,
    x_ref,
    context_ref,
    q_ref,
    o_ref,
    next_q_ref,
    next_o_ref,
    mid_ref,
    out_ref,
    query_ref,
    back_ref,
    context_grad_ref,
    project_ref,
    term_ref,
    inverse_ref,
    total_ref,
):
    step = pl.program_id(0)
    slots = x_ref.shape[0] // NL
    spans = slots // NB

    @pl.when(step == 0)
    def _():
        inverse = inverse_rows(square_ref, full_width)
        for n in range(slots):
            inverse_ref[n * NL : (n + 1) * NL, :] = columns(inverse[n : n + 1, :])
        total_ref[...] = jnp.zeros_like(total_ref)
        term_ref[...] = jnp.zeros_like(term_ref)

    last = lax.broadcasted_iota(jnp.int32, (CH, HD), 0) == CH - 1
    lane = lax.broadcasted_iota(jnp.int32, (1, HD), 1)

    def blocks(own_ref, next_ref, cols):
        own = own_ref[:, cols].astype(f32)
        following = next_ref[:, cols].astype(f32)
        first = jnp.where(last, own[CH - 1 : CH, :], own[CH:, :])
        second = jnp.where(last, own[2 * CH - 1 :, :], following)
        return first, second

    def several(inners):
        heads = [(inner, step * HEADS_PER_STEP + inner) for inner in inners]
        cols = {inner: slice(inner * HD, (inner + 1) * HD) for inner in inners}
        gains = {inner: gain_ref[:, cols[inner]] for inner in inners}
        gates = {inner: jnp.tanh(jnp.full((1, HD), gate_ref[head], f32)) for inner, head in heads}
        pairs = [(inner, n) for inner in inners for n in range(slots)]
        rows = [slice(n * NL, (n + 1) * NL) for n in range(slots)]
        xs = [x_ref[rows[n], cols[i]].astype(f32) for i, n in pairs]
        scaled = [x * inverse_ref[rows[n], :] for x, (i, n) in zip(xs, pairs)]
        normed = [(sc * gains[i]).astype(bf16) for sc, (i, n) in zip(scaled, pairs)]
        keys = [
            jnp.concatenate([no, context_ref[n // NB * CH : (n // NB + 1) * CH, cols[i]]], axis=0)
            for no, (i, n) in zip(normed, pairs)
        ]
        powers = [jnp.exp(dot(ke, no, 1, 1) * (1.0 / HD)) for ke, no in zip(keys, normed)]
        totals = [1.0 / jnp.sum(po, axis=0, keepdims=True) for po in powers]
        weights = [po * to for po, to in zip(powers, totals)]
        probs = [we.astype(bf16) for we in weights]
        encoded = [
            (x + dot(pr, ke, 0, 0)).astype(bf16) for x, pr, ke in zip(xs, probs, keys)
        ]
        items = []
        for inner in inners:
            q_blocks = blocks(q_ref, next_q_ref, cols[inner])
            o_blocks = blocks(o_ref, next_o_ref, cols[inner])
            for span in range(spans):
                first = inners.index(inner) * slots + span * NB
                items.append((
                    q_blocks[span].astype(bf16), o_blocks[span],
                    jnp.concatenate(encoded[first : first + NB], axis=0),
                    counts_ref[span], gates[inner],
                ))
        outputs, query_grads, span_grads, terms = cross(items)
        grads = [
            span_grads[k // NB][k % NB * NL : (k % NB + 1) * NL, :] for k in range(len(pairs))
        ]
        grad_rounded = [gr.astype(bf16) for gr in grads]
        grad_weights = [dot(ke, gr, 1, 1) for ke, gr in zip(keys, grad_rounded)]
        offsets = [jnp.sum(we * gw, axis=0, keepdims=True) for we, gw in zip(weights, grad_weights)]
        score_grads = [
            (we * (gw - of) * (1.0 / HD)).astype(bf16)
            for we, gw, of in zip(weights, grad_weights, offsets)
        ]
        key_grads = [
            dot(
                jnp.concatenate([sg, pr], axis=1),
                jnp.concatenate([no, gr], axis=0),
                1,
                0,
            )
            for sg, pr, no, gr in zip(score_grads, probs, normed, grad_rounded)
        ]
        gained = [
            (dot(sg, ke, 0, 0) + kg[:NL, :]) * gains[i]
            for sg, ke, kg, (i, n) in zip(score_grads, keys, key_grads, pairs)
        ]
        sums = [None] * slots
        for k, (i, n) in enumerate(pairs):
            product = gained[k] * scaled[k]
            sums[n] = product if sums[n] is None else sums[n] + product
            mid_ref[rows[n], cols[i]] = grads[k] + inverse_ref[rows[n], :] * gained[k]
            if n % NB == NB - 1:
                context_grad_ref[n // NB * CH : (n // NB + 1) * CH, cols[i]] = (
                    key_grads[k - 1][NL:, :] + key_grads[k][NL:, :]
                ).astype(bf16)
        for n in range(slots):
            total_ref[rows[n], :] += sums[n]
        result = jnp.zeros((1, HD), f32)
        for at, (inner, head) in enumerate(heads):
            chosen = slice(at * spans, (at + 1) * spans)
            for place, (target, pair) in enumerate(
                ((out_ref, outputs[chosen]), (query_ref, query_grads[chosen]))
            ):
                first, second = pair
                target[0:CH, cols[inner]] = jnp.broadcast_to(first[CH - 1 :, :], (CH, HD)).astype(bf16)
                target[CH:, cols[inner]] = jnp.where(last, second[CH - 1 :, :], first).astype(bf16)
                back_ref[place * CH : (place + 1) * CH, cols[inner]] = second.astype(bf16)
            value = jnp.sum(terms[at * spans] + terms[at * spans + 1], axis=-1, keepdims=True)
            result = result + jnp.where(lane == head, value, 0.0)
        return result

    for at in range(0, HEADS_PER_STEP, SIDE_BY_SIDE):
        term_ref[...] += several(list(range(at, at + SIDE_BY_SIDE)))

    @pl.when(step == pl.num_programs(0) - 1)
    def _():
        for n in range(slots):
            row = row_sums(total_ref[n * NL : (n + 1) * NL, :])
            for device in range(project_ref.shape[0]):
                project_ref[device, n : n + 1, :] = row


def main_part(own_counts, head_gate, squares_all, gain, x, context, queries, out_grad, arrived, full_width):
    rows, width = x.shape
    heads = width // HD
    part = HEADS_PER_STEP * HD
    tokens = queries.shape[0]

    def tall(size, at=0):
        return pl.BlockSpec((size, part), lambda h: (at, h))

    smem = pl.BlockSpec(memory_space=pltpu.SMEM)
    whole = pl.BlockSpec(squares_all.shape, lambda h: (0, 0, 0))
    token_shape = jax.ShapeDtypeStruct((tokens, width), bf16)
    return pl.pallas_call(
        functools.partial(main_kernel, full_width),
        grid=(heads // HEADS_PER_STEP,),
        in_specs=[
            smem,
            smem,
            whole,
            pl.BlockSpec((1, part), lambda h: (0, h)),
            tall(rows),
            tall(tokens),
            tall(tokens),
            tall(tokens),
            tall(CH),
            tall(CH, 1),
        ],
        out_specs=[
            tall(rows),
            tall(tokens),
            tall(tokens),
            tall(tokens),
            tall(tokens),
            whole,
            pl.BlockSpec((1, HD), lambda h: (0, 0)),
        ],
        out_shape=[
            jax.ShapeDtypeStruct((rows, width), f32),
            token_shape,
            token_shape,
            token_shape,
            token_shape,
            jax.ShapeDtypeStruct(squares_all.shape, f32),
            jax.ShapeDtypeStruct((1, HD), f32),
        ],
        scratch_shapes=[pltpu.VMEM((rows, HD), f32), pltpu.VMEM((rows, HD), f32)],
        compiler_params=pltpu.CompilerParams(vmem_limit_bytes=VMEM_LIMIT),
        cost_estimate=cost(8 * 10**9, 10**7),
    )(own_counts, head_gate, squares_all, gain, x, context, queries, out_grad, arrived, arrived)


def final_kernel(
    full_width,
    square_ref,
    project_ref,
    x_ref,
    mid_ref,
    out_in_ref,
    query_in_ref,
    ret_out_ref,
    ret_query_ref,
    grad_ref,
    out_ref,
    query_ref,
    factor_ref,
):
    step = pl.program_id(0)
    slots = x_ref.shape[0] // NL

    @pl.when(step == 0)
    def _():
        inverse = inverse_rows(square_ref, full_width)
        project = (project_ref[0] + project_ref[1]) + (project_ref[2] + project_ref[3])
        factor = inverse * inverse * (project / full_width)
        for n in range(slots):
            factor_ref[n * NL : (n + 1) * NL, :] = columns(factor[n : n + 1, :])

    width = x_ref.shape[1]
    factor = factor_ref[...]
    for at in range(0, width, HD):
        cols = slice(at, at + HD)
        x = x_ref[:, cols].astype(f32)
        grad_ref[:, cols] = (mid_ref[:, cols] - x * factor).astype(bf16)
    last = lax.broadcasted_iota(jnp.int32, (CH, width), 0) == CH - 1
    for own, back, target in (
        (out_in_ref, ret_out_ref, out_ref),
        (query_in_ref, ret_query_ref, query_ref),
    ):
        own_rows = own[...].astype(f32)
        target[...] = jnp.where(last, own_rows, back[...].astype(f32)).astype(bf16)


def final(squares_all, projects_all, x, mid, out, query, returned, full_width):
    rows, width = x.shape
    tokens = out.shape[0]
    part = 2 * HD
    whole = pl.BlockSpec(squares_all.shape, lambda i: (0, 0, 0))
    tall = pl.BlockSpec((rows, part), lambda i: (0, i))
    half = pl.BlockSpec((CH, part), lambda i: (0, i))
    return pl.pallas_call(
        functools.partial(final_kernel, full_width),
        grid=(width // part,),
        in_specs=[
            whole,
            whole,
            tall,
            tall,
            half,
            half,
            half,
            pl.BlockSpec((CH, part), lambda i: (1, i)),
        ],
        out_specs=[tall, half, half],
        out_shape=[
            jax.ShapeDtypeStruct((rows, width), bf16),
            jax.ShapeDtypeStruct((tokens, width), bf16),
            jax.ShapeDtypeStruct((tokens, width), bf16),
        ],
        scratch_shapes=[pltpu.VMEM((rows, HD), f32)],
        input_output_aliases={4: 1, 5: 2},
        compiler_params=pltpu.CompilerParams(vmem_limit_bytes=VMEM_LIMIT),
        cost_estimate=cost(4 * rows * width, 8 * rows * width),
    )(squares_all, projects_all, x, mid, out, query, returned, returned)


def shards(queries, span_state, neigh_state, counts, norm_gain, head_gate, out_grad):
    head_count = head_gate.shape[0]
    width = queries.shape[1]
    row_count = queries.shape[0]
    span_count = row_count // CH
    ranks = lax.axis_size("tensor")
    full_width = float(ranks * width)
    lines = lax.axis_size("dp")

    local_squares, pack = squares(neigh_state, queries, out_grad, ranks)
    arrived = lax.ppermute(pack, "dp", [(i, i - 1) for i in range(1, lines)])
    squares_all = lax.all_to_all(local_squares, "tensor", 0, 0, tiled=True)
    gain = norm_gain[None, :]
    first_span = lax.axis_index("dp") * span_count
    own_counts = lax.dynamic_slice_in_dim(counts.reshape(-1), first_span, span_count)
    mid, out, query, back, context_grad, local_project, term = main_part(
        own_counts, head_gate, squares_all, gain, neigh_state, span_state, queries, out_grad,
        arrived, full_width,
    )
    everyone = lax.axis_size("group") * lines
    gathered = lax.all_to_all(
        jnp.broadcast_to(term, (everyone, HD)), ("group", "dp"), 0, 0, tiled=True
    )
    returned = lax.ppermute(back, "dp", [(i, i + 1) for i in range(lines - 1)])
    projects_all = lax.all_to_all(local_project, "tensor", 0, 0, tiled=True)
    summed = jnp.sum(gathered, axis=0)
    neighbour_grad, out, query = final(
        squares_all, projects_all, neigh_state, mid, out, query, returned, full_width
    )
    gate_tanh = jnp.tanh(head_gate)
    total_tokens = everyone * row_count
    gate_grad = (1.0 - gate_tanh * gate_tanh) * summed[:head_count] / math.sqrt(total_tokens)
    return out, query, context_grad, neighbour_grad, gate_grad


def solution(mesh):
    rows = P(("group", "dp"), "tensor")
    return jax.shard_map(
        shards,
        mesh=mesh,
        in_specs=(rows, rows, rows, P("group", None), P("tensor"), P("tensor"), rows),
        out_specs=(rows, rows, rows, rows, P("tensor")),
        check_vma=False,
    )
```

time: 109 us -> 75.9 us (0.70); the launches traced: 107 us -> 75.4 us
  Pallas kernels: 37.9 us -> 15.7 us
  blocking collectives: 12.4 us -> 0 us
  waiting for transfers between devices: 7.77 us -> 19.2 us
  local copies, waits for them, and re-layouts: 11.2 us -> 3.35 us
    pallas_call x2 -> x1, Pallas kernels: 31.3 us -> 8.4 us  [main_part(): pl.pallas_call(functools.partial(main_kernel, full_width), grid=(heads //...]
    ppermute x2 -> x0, starting transfers between devices: 18.2 us -> none  [shards(): lax.ppermute(summed, 'group', [(i, i ^ step) for i in range(count)])]
    all_to_all x0 -> x1, starting transfers between devices: none -> 17.1 us  [shards(): lax.all_to_all(jnp.broadcast_to(term, (everyone, HD)), ('group', 'dp'), 0...]
    all_to_all x1 -> x0, blocking collectives: 12.4 us -> none  [shards(): lax.all_to_all(jnp.broadcast_to(term, (lines, HD)), 'dp', 0, 0, tiled=True)]
    all_to_all x0 -> x1, waiting for transfers between devices: none -> 11.9 us  [shards(): lax.all_to_all(jnp.broadcast_to(term, (everyone, HD)), ('group', 'dp'), 0...]
    unnamed x30 -> x12, local copies, waits for them, and re-layouts: 11.1 us -> 1.43 us
    broadcast_in_dim x1, local copies, waits for them, and re-layouts: 0.01 us -> 1.33 us  [shards(): jnp.broadcast_to(term, (everyone, HD))]
  transfers between devices with their start and end apart: 6 -> 5, of which waited for: 2 -> 3; matrix products, arithmetic and copies ran while one was open for 1% -> 2% of each run, Pallas kernels for 11% -> 0%
where the time goes in v2:
time: 75.9 us; the launch traced here: 75.4 us
  starting transfers between devices  35.9 us (47%)
  waiting for transfers between devices  19.2 us (25%)
  Pallas kernels  15.7 us (21%)
  local copies, waits for them, and re-layouts  3.35 us (4%)
    all_to_all x1, starting transfers between devices, shards(): lax.all_to_all(jnp.broadcast_to(term, (everyone, HD)), ('group', 'dp'), 0...  17.1 us
    all_to_all x1, waiting for transfers between devices, shards(): lax.all_to_all(jnp.broadcast_to(term, (everyone, HD)), ('group', 'dp'), 0...  11.9 us
    ppermute x1, starting transfers between devices, shards(): arrived = lax.ppermute(pack, 'dp', [(i, i - 1) for i in range(1, lines)])  8.77 us
    pallas_call x1, Pallas kernels, main_part(): pl.pallas_call(functools.partial(main_kernel, full_width), grid=(heads //...  8.4 us
    pallas_call x1, Pallas kernels, final(): pl.pallas_call(functools.partial(final_kernel, full_width), grid=(width /...  4.12 us
    all_to_all x1, waiting for transfers between devices, shards(): squares_all = lax.all_to_all(local_squares, 'tensor', 0, 0, tiled=True)  3.67 us
    all_to_all x1, waiting for transfers between devices, shards(): projects_all = lax.all_to_all(local_project, 'tensor', 0, 0, tiled=True)  3.57 us
    ppermute x1, starting transfers between devices, shards(): returned = lax.ppermute(back, 'dp', [(i, i + 1) for i in range(lines - 1)])  3.54 us
  transfers between devices with their start and end apart: 5, of which 3 were waited for; matrix products, arithmetic and copies ran while one was open for 2% of the time, Pallas kernels for 0%

profile of v2, /device:TPU:1, one launch (start us, length us, event | category | flops | bytes accessed | tf_op | source)
XLA Modules:
  0.0 75.4 jit_solution(12016802053939329108)
XLA Ops:
  0.6 0.0 copy-start
  0.6 3.2 %shard_map.110 = (f32[4,4,128]{2,1,0:T(4,128)}, bf16[128,1024]{1,0:T(8,128)(2,1)}) custom-call(bf16[512,1024]{1,0:T(8,128)(2,1)} %x_ref.5, bf16[128,1024]{1,0:T(8,128)(2,1)} %q_ref.3, bf16[128,1024]{1,0:T(8,128)(2,1)} %o_ref.3), custom_call_target="tpu_custom_call" | custom-call | flops 1048576 | bytes 1048576 | tf_op jit(solution)/shard_map/pallas_call | solution.py:70
  3.8 8.8 %collective-permute-start = (bf16[128,1024]{1,0:T(8,128)(2,1)}, bf16[128,1024]{1,0:T(8,128)(2,1)S(1)}, u32[]{:S(2)}, u32[]{:S(2)}) collective-permute-start(bf16[128,1024]{1,0:T(8,128)(2,1)} %get-tuple-element.18), channel_id=1, source_target_pairs={{4,0},{8,4},{12,8},{16,12},{20,16},{24,20},{28,24},{32,28},{36,32}... | collective-permute-start | bytes 786440 | tf_op jit(solution)/shard_map/ppermute | solution.py:391
  12.6 3.3 %all-to-all-start = ((f32[4,4,128]{2,1,0:T(4,128)}), f32[4,4,128]{2,1,0:T(4,128)S(1)}, u32[]{:S(2)}, u32[]{:S(2)}) async-start(f32[4,4,128]{2,1,0:T(4,128)} %get-tuple-element.17), calls=%async_computation | async-start | bytes 16384 | tf_op jit(solution)/shard_map/all_to_all | solution.py:392
  15.9 0.0 copy-done
  15.9 0.6 dynamic-slice_bitcast_fusion.counts_ref
  16.5 3.7 %all-to-all-done.square_ref = f32[4,4,128]{2,1,0:T(4,128)S(1)} async-done(((f32[4,4,128]{2,1,0:T(4,128)}), f32[4,4,128]{2,1,0:T(4,128)S(1)}, u32[]{:S(2)}, u32[]{:S(2)}) %all-to-all-start) | async-done | bytes 8224 | tf_op jit(solution)/shard_map/all_to_all | solution.py:392
  20.1 0.0 copy-start.2
  20.1 0.0 collective-permute-done.next_q_ref.next_o_ref
  20.1 0.0 copy-start.4
  20.1 0.6 copy-done.2
  20.7 0.1 copy-done.4
  20.8 0.0 copy-start.5
  20.8 8.4 %shard_map.111 = (f32[512,1024]{1,0:T(8,128)}, bf16[128,1024]{1,0:T(8,128)(2,1)}, bf16[128,1024]{1,0:T(8,128)(2,1)}, bf16[128,1024]{1,0:T(8,128)(2,1)}, bf16[128...) custom-call(s32[2]{0:T(128)} %dynamic-slice_bitcast_fusion.counts_ref, f32[8]{0:T(128)} %gate_ref.1, ...), custom_call_target="tpu_custom_call" | custom-call | flops 8000000000 | bytes 10000000 | tf_op jit(solution)/shard_map/pallas_call | solution.py:268
  29.2 1.3 %broadcast_in_dim.9 = f32[128,1,128]{2,1,0:T(1,128)} broadcast(f32[128]{0:T(128)} %bitcast.6), dimensions={2} | broadcast | bytes 66048 | tf_op jit(solution)/shard_map/broadcast_in_dim | solution.py:402
  30.6 17.1 %all-to-all-start.2 = ((f32[128,1,128]{2,1,0:T(1,128)}), f32[128,1,128]{2,1,0:T(1,128)S(1)}, u32[]{:S(2)}, u32[]{:S(2)}) async-start(f32[128,1,128]{2,1,0:T(1,128)} %broadcast_in_dim.9), calls=%async_computation.2 | async-start | bytes 131072 | tf_op jit(solution)/shard_map/all_to_all | solution.py:401
  47.7 3.5 %collective-permute-start.1 = (bf16[128,1024]{1,0:T(8,128)(2,1)}, bf16[128,1024]{1,0:T(8,128)(2,1)S(1)}, u32[]{:S(2)}, u32[]{:S(2)}) collective-permute-start(bf16[128,1024]{1,0:T(8,128)(2,1)} %get-tuple-element.23), channel_id=1, source_target_pairs={{0,4},{4,8},{8,12},{12,16},{16,20},{20,24},{24,28},{28,32},{32,36}... | collective-permute-start | bytes 786440 | tf_op jit(solution)/shard_map/ppermute | solution.py:404
  51.3 11.9 %all-to-all-done.2 = f32[128,1,128]{2,1,0:T(1,128)S(1)} async-done(((f32[128,1,128]{2,1,0:T(1,128)}), f32[128,1,128]{2,1,0:T(1,128)S(1)}, u32[]{:S(2)}, u32[]{:S(2)}) %all-to-all-start.2) | async-done | bytes 65568 | tf_op jit(solution)/shard_map/all_to_all | solution.py:401
  63.2 3.2 %all-to-all-start.1 = ((f32[4,4,128]{2,1,0:T(4,128)}), f32[4,4,128]{2,1,0:T(4,128)S(1)}, u32[]{:S(2)}, u32[]{:S(2)}) async-start(f32[4,4,128]{2,1,0:T(4,128)} %get-tuple-element.19), calls=%async_computation.1 | async-start | bytes 16384 | tf_op jit(solution)/shard_map/all_to_all | solution.py:405
  66.5 0.0 copy-done.5
  66.5 0.5 multiply_multiply_fusion
  67.0 3.6 %all-to-all-done.1.project_ref = f32[4,4,128]{2,1,0:T(4,128)S(1)} async-done(((f32[4,4,128]{2,1,0:T(4,128)}), f32[4,4,128]{2,1,0:T(4,128)S(1)}, u32[]{:S(2)}, u32[]{:S(2)}) %all-to-all-start.1) | async-done | bytes 8224 | tf_op jit(solution)/shard_map/all_to_all | solution.py:405
  70.6 0.0 copy-start.3
  70.6 0.0 collective-permute-done.1.ret_out_ref.ret_query_ref
  70.6 0.0 copy-start.1
  70.6 0.6 copy-done.3
  71.2 0.1 copy-done.1
  71.3 4.1 %shard_map.112 = (bf16[512,1024]{1,0:T(8,128)(2,1)}, bf16[128,1024]{1,0:T(8,128)(2,1)}, bf16[128,1024]{1,0:T(8,128)(2,1)}) custom-call(f32[4,4,128]{2,1,0:T(4,128)} %copy-done.2, f32[4,4,128]{2,1,0:T(4,128)} %copy-done.3, bf16[512,1024]{1,0:T(8,128)(2,1)} %x_ref.5, ...), custom_call_target="tpu_custom_call", output_to_operand_aliasing={{1}: (4, {}), {2}: (5, {})} | custom-call | flops 2097152 | bytes 4194304 | tf_op jit(solution)/shard_map/pallas_call | solution.py:355
  (1 shorter events, 0.0 us)
Async XLA Ops:
  0.6 15.2 %copy-start = (s32[1,64]{1,0:T(1,128)S(1)}, s32[1,64]{1,0:T(1,128)}, u32[]{:S(2)}) copy-start(s32[1,64]{1,0:T(1,128)} %param.10) | copy-start | bytes 772
  3.8 16.3 %collective-permute-start = (bf16[128,1024]{1,0:T(8,128)(2,1)}, bf16[128,1024]{1,0:T(8,128)(2,1)S(1)}, u32[]{:S(2)}, u32[]{:S(2)}) collective-permute-start(bf16[128,1024]{1,0:T(8,128)(2,1)} %get-tuple-element.18), channel_id=1, source_target_pairs={{4,0},{8,4},{12,8},{16,12},{20,16},{24,20},{28,24},{32,28},{36,32}... | collective-permute-start | bytes 786440 | tf_op jit(solution)/shard_map/ppermute | solution.py:391
  12.6 7.5 %all-to-all-start = ((f32[4,4,128]{2,1,0:T(4,128)}), f32[4,4,128]{2,1,0:T(4,128)S(1)}, u32[]{:S(2)}, u32[]{:S(2)}) async-start(f32[4,4,128]{2,1,0:T(4,128)} %get-tuple-element.17), calls=%async_computation | async-start | bytes 16384 | tf_op jit(solution)/shard_map/all_to_all | solution.py:392
  20.1 0.6 copy-start.2
  20.1 0.7 copy-start.4
  20.8 45.6 %copy-start.5 = (f32[8]{0:T(128)S(1)}, f32[8]{0:T(128)}, u32[]{:S(2)}) copy-start(f32[8]{0:T(128)} %gate_ref.1) | copy-start | bytes 100
  30.6 32.6 %all-to-all-start.2 = ((f32[128,1,128]{2,1,0:T(1,128)}), f32[128,1,128]{2,1,0:T(1,128)S(1)}, u32[]{:S(2)}, u32[]{:S(2)}) async-start(f32[128,1,128]{2,1,0:T(1,128)} %broadcast_in_dim.9), calls=%async_computation.2 | async-start | bytes 131072 | tf_op jit(solution)/shard_map/all_to_all | solution.py:401
  47.7 22.9 %collective-permute-start.1 = (bf16[128,1024]{1,0:T(8,128)(2,1)}, bf16[128,1024]{1,0:T(8,128)(2,1)S(1)}, u32[]{:S(2)}, u32[]{:S(2)}) collective-permute-start(bf16[128,1024]{1,0:T(8,128)(2,1)} %get-tuple-element.23), channel_id=1, source_target_pairs={{0,4},{4,8},{8,12},{12,16},{16,20},{20,24},{24,28},{28,32},{32,36}... | collective-permute-start | bytes 786440 | tf_op jit(solution)/shard_map/ppermute | solution.py:404
  63.2 7.4 %all-to-all-start.1 = ((f32[4,4,128]{2,1,0:T(4,128)}), f32[4,4,128]{2,1,0:T(4,128)S(1)}, u32[]{:S(2)}, u32[]{:S(2)}) async-start(f32[4,4,128]{2,1,0:T(4,128)} %get-tuple-element.19), calls=%async_computation.1 | async-start | bytes 16384 | tf_op jit(solution)/shard_map/all_to_all | solution.py:405
  70.6 0.6 copy-start.3
  70.6 0.7 copy-start.1

commit v3 on v2

--- a/solution.py
+++ b/solution.py
@@ -15,9 +15,11 @@
 KEYS = NL + CH
 EPSILON = 1e-05
 MASKED = -1e30
-VMEM_LIMIT = 61 * 1024 * 1024
+VMEM_LIMIT = 60 * 1024 * 1024
 HEADS_PER_STEP = 4
 SIDE_BY_SIDE = 4
+SQUARE_BLOCKS = 2
+FINAL_BLOCKS = 2
 
 f32 = jnp.float32
 bf16 = jnp.bfloat16
@@ -41,44 +43,43 @@
     return jnp.sum(jnp.transpose(block), axis=0, keepdims=True)
 
 
-def inverse_rows(square_ref, full_width):
-    total = (square_ref[0] + square_ref[1]) + (square_ref[2] + square_ref[3])
-    return lax.rsqrt(total / full_width + EPSILON)
+def inverse_rows(square_ref, full_width, at=slice(None)):
+    return lax.rsqrt(square_ref[at, :] / full_width + EPSILON)
 
 
 def squares_kernel(x_ref, q_ref, o_ref, sum_ref, pack_ref):
     step = pl.program_id(0)
     width = x_ref.shape[1]
-    total = jnp.zeros((NL, HD), f32)
-    for at in range(0, width, HD):
-        part = x_ref[:, at : at + HD].astype(f32)
-        total = total + part * part
-    row = row_sums(total)
-    for device in range(sum_ref.shape[0]):
-        sum_ref[device, pl.ds(step, 1), :] = row
+    for n in range(SQUARE_BLOCKS):
+        total = jnp.zeros((NL, HD), f32)
+        for at in range(0, width, HD):
+            part = x_ref[n * NL : (n + 1) * NL, at : at + HD].astype(f32)
+            total = total + part * part
+        sum_ref[pl.ds(step * SQUARE_BLOCKS + n, 1), :] = row_sums(total)
 
     @pl.when(step == 0)
     def _():
-        pack_ref[0:CH, :] = q_ref[...]
-        pack_ref[CH : 2 * CH, :] = o_ref[...]
-
-
-def squares(x, queries, out_grad, ranks):
+        pack_ref[:CH, :] = q_ref[...]
+        pack_ref[CH:, :] = o_ref[...]
+
+
+def squares(x, queries, out_grad):
     rows, width = x.shape
     count = rows // NL
     half = pl.BlockSpec((CH, width), lambda i: (0, 0))
     return pl.pallas_call(
         squares_kernel,
-        grid=(count,),
-        in_specs=[pl.BlockSpec((NL, width), lambda i: (i, 0)), half, half],
+        grid=(count // SQUARE_BLOCKS,),
+        in_specs=[pl.BlockSpec((SQUARE_BLOCKS * NL, width), lambda i: (i, 0)), half, half],
         out_specs=[
-            pl.BlockSpec((ranks, count, NL), lambda i: (0, 0, 0)),
+            pl.BlockSpec((count, NL), lambda i: (0, 0)),
             pl.BlockSpec((2 * CH, width), lambda i: (0, 0)),
         ],
         out_shape=[
-            jax.ShapeDtypeStruct((ranks, count, NL), f32),
+            jax.ShapeDtypeStruct((count, NL), f32),
             jax.ShapeDtypeStruct((2 * CH, width), bf16),
         ],
+        compiler_params=pltpu.CompilerParams(vmem_limit_bytes=VMEM_LIMIT),
         cost_estimate=cost(2 * rows * width, 2 * rows * width),
     )(x, queries, out_grad)
 
@@ -153,6 +154,7 @@
 
     last = lax.broadcasted_iota(jnp.int32, (CH, HD), 0) == CH - 1
     lane = lax.broadcasted_iota(jnp.int32, (1, HD), 1)
+    first_span = lax.axis_index("dp") * spans
 
     def blocks(own_ref, next_ref, cols):
         own = own_ref[:, cols].astype(f32)
@@ -191,7 +193,7 @@
                 items.append((
                     q_blocks[span].astype(bf16), o_blocks[span],
                     jnp.concatenate(encoded[first : first + NB], axis=0),
-                    counts_ref[span], gates[inner],
+                    counts_ref[0, first_span + span], gates[inner],
                 ))
         outputs, query_grads, span_grads, terms = cross(items)
         grads = [
@@ -249,11 +251,11 @@
     def _():
         for n in range(slots):
             row = row_sums(total_ref[n * NL : (n + 1) * NL, :])
-            for device in range(project_ref.shape[0]):
-                project_ref[device, n : n + 1, :] = row
-
-
-def main_part(own_counts, head_gate, squares_all, gain, x, context, queries, out_grad, arrived, full_width):
+            for peer in range(project_ref.shape[0]):
+                project_ref[peer, n : n + 1, :] = row
+
+
+def main_part(counts, head_gate, squares_all, gain, x, context, queries, out_grad, arrived, full_width, ranks):
     rows, width = x.shape
     heads = width // HD
     part = HEADS_PER_STEP * HD
@@ -263,7 +265,7 @@
         return pl.BlockSpec((size, part), lambda h: (at, h))
 
     smem = pl.BlockSpec(memory_space=pltpu.SMEM)
-    whole = pl.BlockSpec(squares_all.shape, lambda h: (0, 0, 0))
+    whole = pl.BlockSpec(squares_all.shape, lambda h: (0, 0))
     token_shape = jax.ShapeDtypeStruct((tokens, width), bf16)
     return pl.pallas_call(
         functools.partial(main_kernel, full_width),
@@ -286,7 +288,7 @@
             tall(tokens),
             tall(tokens),
             tall(tokens),
-            whole,
+            pl.BlockSpec((ranks,) + squares_all.shape, lambda h: (0, 0, 0)),
             pl.BlockSpec((1, HD), lambda h: (0, 0)),
         ],
         out_shape=[
@@ -295,13 +297,13 @@
             token_shape,
             token_shape,
             token_shape,
-            jax.ShapeDtypeStruct(squares_all.shape, f32),
+            jax.ShapeDtypeStruct((ranks,) + squares_all.shape, f32),
             jax.ShapeDtypeStruct((1, HD), f32),
         ],
         scratch_shapes=[pltpu.VMEM((rows, HD), f32), pltpu.VMEM((rows, HD), f32)],
         compiler_params=pltpu.CompilerParams(vmem_limit_bytes=VMEM_LIMIT),
         cost_estimate=cost(8 * 10**9, 10**7),
-    )(own_counts, head_gate, squares_all, gain, x, context, queries, out_grad, arrived, arrived)
+    )(counts, head_gate, squares_all, gain, x, context, queries, out_grad, arrived, arrived)
 
 
 def final_kernel(
@@ -314,29 +316,30 @@
     query_in_ref,
     ret_out_ref,
     ret_query_ref,
+    gate_ref,
     grad_ref,
     out_ref,
     query_ref,
-    factor_ref,
+    slope_ref,
+    *,
+    slope_scale,
 ):
     step = pl.program_id(0)
-    slots = x_ref.shape[0] // NL
-
-    @pl.when(step == 0)
-    def _():
-        inverse = inverse_rows(square_ref, full_width)
-        project = (project_ref[0] + project_ref[1]) + (project_ref[2] + project_ref[3])
-        factor = inverse * inverse * (project / full_width)
-        for n in range(slots):
-            factor_ref[n * NL : (n + 1) * NL, :] = columns(factor[n : n + 1, :])
-
+    gate_tanh = jnp.tanh(gate_ref[...])
+    slope_ref[...] = (1.0 - gate_tanh * gate_tanh) * slope_scale
     width = x_ref.shape[1]
-    factor = factor_ref[...]
-    for at in range(0, width, HD):
-        cols = slice(at, at + HD)
-        x = x_ref[:, cols].astype(f32)
-        grad_ref[:, cols] = (mid_ref[:, cols] - x * factor).astype(bf16)
-    last = lax.broadcasted_iota(jnp.int32, (CH, width), 0) == CH - 1
+    for n in range(FINAL_BLOCKS):
+        row = pl.ds(step * FINAL_BLOCKS + n, 1)
+        inverse = inverse_rows(square_ref, full_width, row)
+        one, two, three, four = (project_ref[at, row, :] for at in range(4))
+        project = (one + two) + (three + four)
+        factor = columns(inverse * inverse * (project / full_width))
+        rows = slice(n * NL, (n + 1) * NL)
+        for at in range(0, width, HD):
+            cols = slice(at, at + HD)
+            x = x_ref[rows, cols].astype(f32)
+            grad_ref[rows, cols] = (mid_ref[rows, cols] - x * factor).astype(bf16)
+    last = lax.broadcasted_iota(jnp.int32, (CH, out_ref.shape[1]), 0) == CH - 1
     for own, back, target in (
         (out_in_ref, ret_out_ref, out_ref),
         (query_in_ref, ret_query_ref, query_ref),
@@ -345,71 +348,82 @@
         target[...] = jnp.where(last, own_rows, back[...].astype(f32)).astype(bf16)
 
 
-def final(squares_all, projects_all, x, mid, out, query, returned, full_width):
+def final(
+    squares_all, projects_all, x, mid, out, query, returned, head_gate, full_width, scale
+):
     rows, width = x.shape
     tokens = out.shape[0]
-    part = 2 * HD
-    whole = pl.BlockSpec(squares_all.shape, lambda i: (0, 0, 0))
-    tall = pl.BlockSpec((rows, part), lambda i: (0, i))
+    count = rows // NL // FINAL_BLOCKS
+    part = width // count
+    gate = pl.BlockSpec(head_gate.shape, lambda i: (0, 0))
+    whole = pl.BlockSpec(squares_all.shape, lambda i: (0, 0))
+    rowwise = pl.BlockSpec((FINAL_BLOCKS * NL, width), lambda i: (i, 0))
     half = pl.BlockSpec((CH, part), lambda i: (0, i))
     return pl.pallas_call(
-        functools.partial(final_kernel, full_width),
-        grid=(width // part,),
+        functools.partial(final_kernel, full_width, slope_scale=scale),
+        grid=(count,),
         in_specs=[
             whole,
-            whole,
-            tall,
-            tall,
+            pl.BlockSpec(projects_all.shape, lambda i: (0, 0, 0)),
+            rowwise,
+            rowwise,
             half,
             half,
             half,
             pl.BlockSpec((CH, part), lambda i: (1, i)),
-        ],
-        out_specs=[tall, half, half],
+            gate,
+        ],
+        out_specs=[rowwise, half, half, gate],
         out_shape=[
             jax.ShapeDtypeStruct((rows, width), bf16),
             jax.ShapeDtypeStruct((tokens, width), bf16),
             jax.ShapeDtypeStruct((tokens, width), bf16),
-        ],
-        scratch_shapes=[pltpu.VMEM((rows, HD), f32)],
+            jax.ShapeDtypeStruct(head_gate.shape, f32),
+        ],
         input_output_aliases={4: 1, 5: 2},
         compiler_params=pltpu.CompilerParams(vmem_limit_bytes=VMEM_LIMIT),
         cost_estimate=cost(4 * rows * width, 8 * rows * width),
-    )(squares_all, projects_all, x, mid, out, query, returned, returned)
+    )(squares_all, projects_all, x, mid, out, query, returned, returned, head_gate)
+
+
+def gate_kernel(slope_ref, terms_ref, grad_ref):
+    heads = grad_ref.shape[1]
+    total = jnp.sum(terms_ref[...], axis=0)
+    grad_ref[...] = slope_ref[...] * total[:, :heads]
+
+
+def gate_part(slope, terms):
+    return pl.pallas_call(
+        gate_kernel,
+        out_shape=jax.ShapeDtypeStruct(slope.shape, f32),
+        compiler_params=pltpu.CompilerParams(vmem_limit_bytes=16 * 1024 * 1024),
+        cost_estimate=cost(1000, 1000),
+    )(slope, terms)
 
 
 def shards(queries, span_state, neigh_state, counts, norm_gain, head_gate, out_grad):
     head_count = head_gate.shape[0]
     width = queries.shape[1]
     row_count = queries.shape[0]
-    span_count = row_count // CH
-    ranks = lax.axis_size("tensor")
-    full_width = float(ranks * width)
+    full_width = float(lax.axis_size("tensor") * width)
     lines = lax.axis_size("dp")
 
-    local_squares, pack = squares(neigh_state, queries, out_grad, ranks)
+    local_squares, pack = squares(neigh_state, queries, out_grad)
+    squares_all = lax.psum(local_squares, "tensor")
     arrived = lax.ppermute(pack, "dp", [(i, i - 1) for i in range(1, lines)])
-    squares_all = lax.all_to_all(local_squares, "tensor", 0, 0, tiled=True)
-    gain = norm_gain[None, :]
-    first_span = lax.axis_index("dp") * span_count
-    own_counts = lax.dynamic_slice_in_dim(counts.reshape(-1), first_span, span_count)
-    mid, out, query, back, context_grad, local_project, term = main_part(
-        own_counts, head_gate, squares_all, gain, neigh_state, span_state, queries, out_grad,
-        arrived, full_width,
+    mid, out, query, back, context_grad, project, term = main_part(
+        counts, head_gate, squares_all, norm_gain[None, :], neigh_state, span_state, queries,
+        out_grad, arrived, full_width, lax.axis_size("tensor"),
     )
-    everyone = lax.axis_size("group") * lines
-    gathered = lax.all_to_all(
-        jnp.broadcast_to(term, (everyone, HD)), ("group", "dp"), 0, 0, tiled=True
+    projects_all = lax.all_to_all(project, "tensor", 0, 0, tiled=True)
+    returned = lax.ppermute(back, "dp", [(i, i + 1) for i in range(lines - 1)])
+    line_terms = jnp.broadcast_to(lax.psum(term, "group"), (lines, 1, HD))
+    terms = lax.all_to_all(line_terms, "dp", 0, 0, tiled=True)
+    neighbour_grad, out, query, slope = final(
+        squares_all, projects_all, neigh_state, mid, out, query, returned, head_gate[None, :],
+        full_width, 1.0 / math.sqrt(lax.axis_size("group") * lines * row_count),
     )
-    returned = lax.ppermute(back, "dp", [(i, i + 1) for i in range(lines - 1)])
-    projects_all = lax.all_to_all(local_project, "tensor", 0, 0, tiled=True)
-    summed = jnp.sum(gathered, axis=0)
-    neighbour_grad, out, query = final(
-        squares_all, projects_all, neigh_state, mid, out, query, returned, full_width
-    )
-    gate_tanh = jnp.tanh(head_gate)
-    total_tokens = everyone * row_count
-    gate_grad = (1.0 - gate_tanh * gate_tanh) * summed[:head_count] / math.sqrt(total_tokens)
+    gate_grad = gate_part(slope, terms)[0]
     return out, query, context_grad, neighbour_grad, gate_grad
 
 

time: 75.9 us -> 70.3 us (0.926)
  blocking collectives: 0 us -> 25.6 us
  waiting for transfers between devices: 19.2 us -> 3.46 us
  starting transfers between devices: 35.9 us -> 23.4 us
  Pallas kernels: 15.7 us -> 14.1 us
    psum x0 -> x2, blocking collectives: none -> 25.6 us  [the longest x1 18.9 us: shards(): line_terms = jnp.broadcast_to(lax.psum(term, 'group'), (lines, 1, HD))]
    all_to_all x3 -> x2, waiting for transfers between devices: 19.2 us -> 3.46 us  [the longest x1 3.45 us: shards(): terms = lax.all_to_all(line_terms, 'dp', 0, 0, tiled=True)]
    all_to_all x3 -> x2, starting transfers between devices: 23.6 us -> 12 us  [the longest x1 8.8 us: shards(): terms = lax.all_to_all(line_terms, 'dp', 0, 0, tiled=True)]
    pallas_call x2 -> x3, Pallas kernels: 7.27 us -> 5.77 us  [the longest x1 3.02 us: final(): pl.pallas_call(functools.partial(final_kernel, full_width, slope_scale=sc...]
    ppermute x1, starting transfers between devices: 3.54 us -> 2.56 us  [shards(): returned = lax.ppermute(back, 'dp', [(i, i + 1) for i in range(lines - 1)])]
    unnamed x12 -> x8, local copies, waits for them, and re-layouts: 1.43 us -> 2.04 us
  transfers between devices with their start and end apart: 5 -> 4, of which waited for: 3 -> 1; matrix products, arithmetic and copies ran while one was open for 2% -> 1% of each run, Pallas kernels for 0% -> 4%
where the time goes in v3:
time: 70.3 us; the launch traced here: 69.9 us
  blocking collectives  25.6 us (36%)
  starting transfers between devices  23.4 us (33%)
  Pallas kernels  14.1 us (20%)
  waiting for transfers between devices  3.46 us (5%)
  local copies, waits for them, and re-layouts  2.65 us (4%)
    psum x1, blocking collectives, shards(): line_terms = jnp.broadcast_to(lax.psum(term, 'group'), (lines, 1, HD))  18.9 us
    all_to_all x1, starting transfers between devices, shards(): terms = lax.all_to_all(line_terms, 'dp', 0, 0, tiled=True)  8.8 us
    ppermute x1, starting transfers between devices, shards(): arrived = lax.ppermute(pack, 'dp', [(i, i - 1) for i in range(1, lines)])  8.77 us
    pallas_call x1, Pallas kernels, main_part(): pl.pallas_call(functools.partial(main_kernel, full_width), grid=(heads //...  8.35 us
    psum x1, blocking collectives, shards(): squares_all = lax.psum(local_squares, 'tensor')  6.7 us
    all_to_all x1, waiting for transfers between devices, shards(): terms = lax.all_to_all(line_terms, 'dp', 0, 0, tiled=True)  3.45 us
    all_to_all x1, starting transfers between devices, shards(): projects_all = lax.all_to_all(project, 'tensor', 0, 0, tiled=True)  3.25 us
    pallas_call x1, Pallas kernels, final(): pl.pallas_call(functools.partial(final_kernel, full_width, slope_scale=sc...  3.02 us
  transfers between devices with their start and end apart: 4, of which 1 were waited for; matrix products, arithmetic and copies ran while one was open for 1% of the time, Pallas kernels for 4%

profile of v3, /device:TPU:1, one launch (start us, length us, event | category | flops | bytes accessed | tf_op | source)
XLA Modules:
  0.0 69.9 jit_solution(612387074685668795)
XLA Ops:
  0.6 2.2 %shard_map.110 = (f32[4,128]{1,0:T(4,128)}, bf16[128,1024]{1,0:T(8,128)(2,1)}) custom-call(bf16[512,1024]{1,0:T(8,128)(2,1)} %x_ref.5, bf16[128,1024]{1,0:T(8,128)(2,1)} %q_ref.3, bf16[128,1024]{1,0:T(8,128)(2,1)} %o_ref.3), custom_call_target="tpu_custom_call" | custom-call | flops 1048576 | bytes 1048576 | tf_op jit(solution)/shard_map/pallas_call | solution.py:70
  2.8 8.8 %collective-permute-start = (bf16[128,1024]{1,0:T(8,128)(2,1)}, bf16[128,1024]{1,0:T(8,128)(2,1)S(1)}, u32[]{:S(2)}, u32[]{:S(2)}) collective-permute-start(bf16[128,1024]{1,0:T(8,128)(2,1)} %get-tuple-element.19), channel_id=1, source_target_pairs={{4,0},{8,4},{12,8},{16,12},{20,16},{24,20},{28,24},{32,28},{36,32}... | collective-permute-start | bytes 786440 | tf_op jit(solution)/shard_map/ppermute | solution.py:413
  11.6 6.7 %psum.16.square_ref = f32[4,128]{1,0:T(4,128)} all-reduce(f32[4,128]{1,0:T(4,128)} %get-tuple-element.18), channel_id=1, replica_groups=mesh['group'=4,'dp'=32,'tensor'=4] {'tensor'}, use_global_device_ids=true, to_apply=%region_0.0 | all-reduce | flops 512 | bytes 4096 | tf_op jit(solution)/shard_map/psum | solution.py:412
  18.3 0.0 collective-permute-done.next_q_ref.next_o_ref
  18.3 0.0 copy-start.3
  18.3 0.7 %copy-done.3 = bf16[128,1024]{1,0:T(8,128)(2,1)} copy-done((bf16[128,1024]{1,0:T(8,128)(2,1)}, bf16[128,1024]{1,0:T(8,128)(2,1)S(1)}, u32[]{:S(2)}) %copy-start.3) | copy-done | bytes 262168
  19.0 8.3 %shard_map.111 = (f32[512,1024]{1,0:T(8,128)}, bf16[128,1024]{1,0:T(8,128)(2,1)}, bf16[128,1024]{1,0:T(8,128)(2,1)}, bf16[128,1024]{1,0:T(8,128)(2,1)}, bf16[128...) custom-call(s32[1,64]{1,0:T(1,128)} %counts_ref.1, f32[8]{0:T(128)} %gate_ref.1, ...), custom_call_target="tpu_custom_call" | custom-call | flops 8000000000 | bytes 10000000 | tf_op jit(solution)/shard_map/pallas_call | solution.py:270
  27.4 2.6 %collective-permute-start.1 = (bf16[128,1024]{1,0:T(8,128)(2,1)}, bf16[128,1024]{1,0:T(8,128)(2,1)S(1)}, u32[]{:S(2)}, u32[]{:S(2)}) collective-permute-start(bf16[128,1024]{1,0:T(8,128)(2,1)} %get-tuple-element.24), channel_id=1, source_target_pairs={{0,4},{4,8},{8,12},{12,16},{16,20},{20,24},{24,28},{28,32},{32,36}... | collective-permute-start | bytes 786440 | tf_op jit(solution)/shard_map/ppermute | solution.py:419
  29.9 3.2 %all-to-all-start = ((f32[4,4,128]{2,1,0:T(4,128)}), f32[4,4,128]{2,1,0:T(4,128)S(1)}, u32[]{:S(2)}, u32[]{:S(2)}) async-start(f32[4,4,128]{2,1,0:T(4,128)} %get-tuple-element.20), calls=%async_computation | async-start | bytes 16384 | tf_op jit(solution)/shard_map/all_to_all | solution.py:418
  33.2 18.9 %psum.18 = f32[128]{0:T(128)S(1)} all-reduce(f32[128]{0:T(128)} %bitcast.7), channel_id=1, replica_groups=mesh['group'=4,'dp'=32,'tensor'=4] {'group'}, use_global_device_ids=true, to_apply=%region_1.0 | all-reduce | flops 128 | bytes 1024 | tf_op jit(solution)/shard_map/psum | solution.py:420
  52.1 0.0 all-to-all-done.project_ref
  52.1 0.0 copy-start.2
  52.1 0.6 broadcast_in_dim.11
  52.7 8.8 %all-to-all-start.1 = ((f32[32,1,128]{2,1,0:T(1,128)}), f32[32,1,128]{2,1,0:T(1,128)S(1)}, u32[]{:S(2)}, u32[]{:S(2)}) async-start(f32[32,1,128]{2,1,0:T(1,128)} %broadcast_in_dim.11), calls=%async_computation.1 | async-start | bytes 32768 | tf_op jit(solution)/shard_map/all_to_all | solution.py:421
  61.5 0.0 collective-permute-done.1.ret_out_ref.ret_query_ref
  61.5 0.0 copy-start.1
  61.5 0.0 copy-done.2
  61.5 0.7 copy-done.1
  62.2 3.0 %shard_map.112 = (bf16[512,1024]{1,0:T(8,128)(2,1)}, bf16[128,1024]{1,0:T(8,128)(2,1)}, bf16[128,1024]{1,0:T(8,128)(2,1)}, f32[1,8]{1,0:T(1,128)}) custom-call(f32[4,128]{1,0:T(4,128)} %psum.16.square_ref, f32[4,4,128]{2,1,0:T(4,128)} %copy-done.2, bf16[512,1024]{1,0:T(8,128)(2,1)} %x_ref.5, ...), custom_call_target="tpu_custom_call", output_to_operand_aliasing={{1}: (4, {}), {2}: (5, {})} | custom-call | flops 2097152 | bytes 4194304 | tf_op jit(solution)/shard_map/pallas_call | solution.py:362
  65.2 3.5 %all-to-all-done.1.terms_ref = f32[32,1,128]{2,1,0:T(1,128)S(1)} async-done(((f32[32,1,128]{2,1,0:T(1,128)}), f32[32,1,128]{2,1,0:T(1,128)S(1)}, u32[]{:S(2)}, u32[]{:S(2)}) %all-to-all-start.1) | async-done | bytes 16416 | tf_op jit(solution)/shard_map/all_to_all | solution.py:421
  68.7 0.0 copy-start
  68.7 0.7 copy-done
  69.4 0.5 shard_map.113
Async XLA Ops:
  2.8 15.5 %collective-permute-start = (bf16[128,1024]{1,0:T(8,128)(2,1)}, bf16[128,1024]{1,0:T(8,128)(2,1)S(1)}, u32[]{:S(2)}, u32[]{:S(2)}) collective-permute-start(bf16[128,1024]{1,0:T(8,128)(2,1)} %get-tuple-element.19), channel_id=1, source_target_pairs={{4,0},{8,4},{12,8},{16,12},{20,16},{24,20},{28,24},{32,28},{36,32}... | collective-permute-start | bytes 786440 | tf_op jit(solution)/shard_map/ppermute | solution.py:413
  18.3 0.7 %copy-start.3 = (bf16[128,1024]{1,0:T(8,128)(2,1)}, bf16[128,1024]{1,0:T(8,128)(2,1)S(1)}, u32[]{:S(2)}) copy-start(bf16[128,1024]{1,0:T(8,128)(2,1)S(1)} %collective-permute-done.next_q_ref.next_o_ref) | copy-start | bytes 786436
  27.4 34.1 %collective-permute-start.1 = (bf16[128,1024]{1,0:T(8,128)(2,1)}, bf16[128,1024]{1,0:T(8,128)(2,1)S(1)}, u32[]{:S(2)}, u32[]{:S(2)}) collective-permute-start(bf16[128,1024]{1,0:T(8,128)(2,1)} %get-tuple-element.24), channel_id=1, source_target_pairs={{0,4},{4,8},{8,12},{12,16},{16,20},{20,24},{24,28},{28,32},{32,36}... | collective-permute-start | bytes 786440 | tf_op jit(solution)/shard_map/ppermute | solution.py:419
  29.9 22.2 %all-to-all-start = ((f32[4,4,128]{2,1,0:T(4,128)}), f32[4,4,128]{2,1,0:T(4,128)S(1)}, u32[]{:S(2)}, u32[]{:S(2)}) async-start(f32[4,4,128]{2,1,0:T(4,128)} %get-tuple-element.20), calls=%async_computation | async-start | bytes 16384 | tf_op jit(solution)/shard_map/all_to_all | solution.py:418
  52.1 9.4 %copy-start.2 = (f32[4,4,128]{2,1,0:T(4,128)}, f32[4,4,128]{2,1,0:T(4,128)S(1)}, u32[]{:S(2)}) copy-start(f32[4,4,128]{2,1,0:T(4,128)S(1)} %all-to-all-done.project_ref) | copy-start | bytes 24580
  52.7 16.0 %all-to-all-start.1 = ((f32[32,1,128]{2,1,0:T(1,128)}), f32[32,1,128]{2,1,0:T(1,128)S(1)}, u32[]{:S(2)}, u32[]{:S(2)}) async-start(f32[32,1,128]{2,1,0:T(1,128)} %broadcast_in_dim.11), calls=%async_computation.1 | async-start | bytes 32768 | tf_op jit(solution)/shard_map/all_to_all | solution.py:421
  61.5 0.7 copy-start.1
  68.7 0.7 copy-start

commit v4 on v3

--- a/solution.py
+++ b/solution.py
@@ -16,6 +16,8 @@
 EPSILON = 1e-05
 MASKED = -1e30
 VMEM_LIMIT = 60 * 1024 * 1024
+MAIN_LIMIT = 61440 * 1024
+FINAL_LIMIT = 54528 * 1024
 HEADS_PER_STEP = 4
 SIDE_BY_SIDE = 4
 SQUARE_BLOCKS = 2
@@ -88,12 +90,12 @@
     scale = 1.0 / math.sqrt(HD)
     lane = lax.broadcasted_iota(jnp.int32, (CH, NB * NL), 1)
     scores = [dot(block, keys, 1, 1) * scale for block, _, keys, _, _ in items]
-    scores = [jnp.where(lane < it[3] * NL, sc, MASKED) for it, sc in zip(items, scores)]
-    highest = [jnp.max(sc, axis=-1, keepdims=True) for sc in scores]
-    powers = [jnp.exp(sc - hi) for sc, hi in zip(scores, highest)]
-    sums = [jnp.sum(po, axis=-1, keepdims=True) for po in powers]
-    weights = [po * (1.0 / su) for po, su in zip(powers, sums)]
-    rounded = [we.astype(bf16) for we in weights]
+    weights, rounded = [], []
+    for it, score in zip(items, scores):
+        score = jnp.where(lane < it[3] * NL, score, MASKED)
+        powers = jnp.exp(score - jnp.max(score, axis=-1, keepdims=True))
+        weights.append(powers * (1.0 / jnp.sum(powers, axis=-1, keepdims=True)))
+        rounded.append(weights[-1].astype(bf16))
     attended = [dot(ro, it[2], 1, 0) for it, ro in zip(items, rounded)]
     attended = [jnp.where(it[3] > 0, at, 0.0) for it, at in zip(items, attended)]
     att_grad = [jnp.where(it[3] > 0, it[4] * it[1], 0.0) for it in items]
@@ -177,10 +179,12 @@
             jnp.concatenate([no, context_ref[n // NB * CH : (n // NB + 1) * CH, cols[i]]], axis=0)
             for no, (i, n) in zip(normed, pairs)
         ]
-        powers = [jnp.exp(dot(ke, no, 1, 1) * (1.0 / HD)) for ke, no in zip(keys, normed)]
-        totals = [1.0 / jnp.sum(po, axis=0, keepdims=True) for po in powers]
-        weights = [po * to for po, to in zip(powers, totals)]
-        probs = [we.astype(bf16) for we in weights]
+        scores = [dot(ke, no, 1, 1) for ke, no in zip(keys, normed)]
+        weights, probs = [], []
+        for score in scores:
+            powers = jnp.exp(score * (1.0 / HD))
+            weights.append(powers * (1.0 / jnp.sum(powers, axis=0, keepdims=True)))
+            probs.append(weights[-1].astype(bf16))
         encoded = [
             (x + dot(pr, ke, 0, 0)).astype(bf16) for x, pr, ke in zip(xs, probs, keys)
         ]
@@ -201,11 +205,10 @@
         ]
         grad_rounded = [gr.astype(bf16) for gr in grads]
         grad_weights = [dot(ke, gr, 1, 1) for ke, gr in zip(keys, grad_rounded)]
-        offsets = [jnp.sum(we * gw, axis=0, keepdims=True) for we, gw in zip(weights, grad_weights)]
-        score_grads = [
-            (we * (gw - of) * (1.0 / HD)).astype(bf16)
-            for we, gw, of in zip(weights, grad_weights, offsets)
-        ]
+        score_grads = []
+        for we, gw in zip(weights, grad_weights):
+            offset = jnp.sum(we * gw, axis=0, keepdims=True)
+            score_grads.append((we * (gw - offset) * (1.0 / HD)).astype(bf16))
         key_grads = [
             dot(
                 jnp.concatenate([sg, pr], axis=1),
@@ -251,11 +254,10 @@
     def _():
         for n in range(slots):
             row = row_sums(total_ref[n * NL : (n + 1) * NL, :])
-            for peer in range(project_ref.shape[0]):
-                project_ref[peer, n : n + 1, :] = row
-
-
-def main_part(counts, head_gate, squares_all, gain, x, context, queries, out_grad, arrived, full_width, ranks):
+            project_ref[n : n + 1, :] = row
+
+
+def main_part(counts, head_gate, squares_all, gain, x, context, queries, out_grad, arrived, full_width):
     rows, width = x.shape
     heads = width // HD
     part = HEADS_PER_STEP * HD
@@ -288,7 +290,7 @@
             tall(tokens),
             tall(tokens),
             tall(tokens),
-            pl.BlockSpec((ranks,) + squares_all.shape, lambda h: (0, 0, 0)),
+            whole,
             pl.BlockSpec((1, HD), lambda h: (0, 0)),
         ],
         out_shape=[
@@ -297,11 +299,11 @@
             token_shape,
             token_shape,
             token_shape,
-            jax.ShapeDtypeStruct((ranks,) + squares_all.shape, f32),
+            jax.ShapeDtypeStruct(squares_all.shape, f32),
             jax.ShapeDtypeStruct((1, HD), f32),
         ],
         scratch_shapes=[pltpu.VMEM((rows, HD), f32), pltpu.VMEM((rows, HD), f32)],
-        compiler_params=pltpu.CompilerParams(vmem_limit_bytes=VMEM_LIMIT),
+        compiler_params=pltpu.CompilerParams(vmem_limit_bytes=MAIN_LIMIT),
         cost_estimate=cost(8 * 10**9, 10**7),
     )(counts, head_gate, squares_all, gain, x, context, queries, out_grad, arrived, arrived)
 
@@ -317,22 +319,23 @@
     ret_out_ref,
     ret_query_ref,
     gate_ref,
+    terms_ref,
     grad_ref,
     out_ref,
     query_ref,
-    slope_ref,
+    gate_grad_ref,
     *,
-    slope_scale,
+    scale,
 ):
     step = pl.program_id(0)
     gate_tanh = jnp.tanh(gate_ref[...])
-    slope_ref[...] = (1.0 - gate_tanh * gate_tanh) * slope_scale
+    summed = jnp.sum(terms_ref[...], axis=0)[:, : gate_tanh.shape[1]]
+    gate_grad_ref[...] = (1.0 - gate_tanh * gate_tanh) * summed * scale
     width = x_ref.shape[1]
     for n in range(FINAL_BLOCKS):
         row = pl.ds(step * FINAL_BLOCKS + n, 1)
         inverse = inverse_rows(square_ref, full_width, row)
-        one, two, three, four = (project_ref[at, row, :] for at in range(4))
-        project = (one + two) + (three + four)
+        project = project_ref[row, :]
         factor = columns(inverse * inverse * (project / full_width))
         rows = slice(n * NL, (n + 1) * NL)
         for at in range(0, width, HD):
@@ -349,7 +352,7 @@
 
 
 def final(
-    squares_all, projects_all, x, mid, out, query, returned, head_gate, full_width, scale
+    squares_all, projects_all, x, mid, out, query, returned, head_gate, terms, full_width, scale
 ):
     rows, width = x.shape
     tokens = out.shape[0]
@@ -360,11 +363,11 @@
     rowwise = pl.BlockSpec((FINAL_BLOCKS * NL, width), lambda i: (i, 0))
     half = pl.BlockSpec((CH, part), lambda i: (0, i))
     return pl.pallas_call(
-        functools.partial(final_kernel, full_width, slope_scale=scale),
+        functools.partial(final_kernel, full_width, scale=scale),
         grid=(count,),
         in_specs=[
             whole,
-            pl.BlockSpec(projects_all.shape, lambda i: (0, 0, 0)),
+            pl.BlockSpec(projects_all.shape, lambda i: (0, 0)),
             rowwise,
             rowwise,
             half,
@@ -372,6 +375,7 @@
             half,
             pl.BlockSpec((CH, part), lambda i: (1, i)),
             gate,
+            pl.BlockSpec(terms.shape, lambda i: (0, 0, 0)),
         ],
         out_specs=[rowwise, half, half, gate],
         out_shape=[
@@ -381,28 +385,12 @@
             jax.ShapeDtypeStruct(head_gate.shape, f32),
         ],
         input_output_aliases={4: 1, 5: 2},
-        compiler_params=pltpu.CompilerParams(vmem_limit_bytes=VMEM_LIMIT),
+        compiler_params=pltpu.CompilerParams(vmem_limit_bytes=FINAL_LIMIT),
         cost_estimate=cost(4 * rows * width, 8 * rows * width),
-    )(squares_all, projects_all, x, mid, out, query, returned, returned, head_gate)
-
-
-def gate_kernel(slope_ref, terms_ref, grad_ref):
-    heads = grad_ref.shape[1]
-    total = jnp.sum(terms_ref[...], axis=0)
-    grad_ref[...] = slope_ref[...] * total[:, :heads]
-
-
-def gate_part(slope, terms):
-    return pl.pallas_call(
-        gate_kernel,
-        out_shape=jax.ShapeDtypeStruct(slope.shape, f32),
-        compiler_params=pltpu.CompilerParams(vmem_limit_bytes=16 * 1024 * 1024),
-        cost_estimate=cost(1000, 1000),
-    )(slope, terms)
+    )(squares_all, projects_all, x, mid, out, query, returned, returned, head_gate, terms)
 
 
 def shards(queries, span_state, neigh_state, counts, norm_gain, head_gate, out_grad):
-    head_count = head_gate.shape[0]
     width = queries.shape[1]
     row_count = queries.shape[0]
     full_width = float(lax.axis_size("tensor") * width)
@@ -413,18 +401,19 @@
     arrived = lax.ppermute(pack, "dp", [(i, i - 1) for i in range(1, lines)])
     mid, out, query, back, context_grad, project, term = main_part(
         counts, head_gate, squares_all, norm_gain[None, :], neigh_state, span_state, queries,
-        out_grad, arrived, full_width, lax.axis_size("tensor"),
+        out_grad, arrived, full_width,
     )
-    projects_all = lax.all_to_all(project, "tensor", 0, 0, tiled=True)
     returned = lax.ppermute(back, "dp", [(i, i + 1) for i in range(lines - 1)])
     line_terms = jnp.broadcast_to(lax.psum(term, "group"), (lines, 1, HD))
+    line_terms, project = lax.optimization_barrier((line_terms, project))
     terms = lax.all_to_all(line_terms, "dp", 0, 0, tiled=True)
-    neighbour_grad, out, query, slope = final(
+    projects_all = lax.psum(project, "tensor")
+    neighbour_grad, out, query, gate_grad = final(
         squares_all, projects_all, neigh_state, mid, out, query, returned, head_gate[None, :],
+        terms,
         full_width, 1.0 / math.sqrt(lax.axis_size("group") * lines * row_count),
     )
-    gate_grad = gate_part(slope, terms)[0]
-    return out, query, context_grad, neighbour_grad, gate_grad
+    return out, query, context_grad, neighbour_grad, gate_grad[0]
 
 
 def solution(mesh):

time: 70.3 us -> 68.9 us (0.980)
  blocking collectives: 25.6 us -> 32.5 us
  starting transfers between devices: 23.4 us -> 19.9 us
  waiting for transfers between devices: 3.46 us -> 0.52 us
  local copies, waits for them, and re-layouts: 2.65 us -> 1.33 us
    psum x0 -> x1, blocking collectives: none -> 6.6 us  [shards(): projects_all = lax.psum(project, 'tensor')]
    all_to_all x1 -> x0, starting transfers between devices: 3.25 us -> none  [shards(): projects_all = lax.all_to_all(project, 'tensor', 0, 0, tiled=True)]
    all_to_all x1, waiting for transfers between devices: 3.45 us -> 0.51 us  [shards(): terms = lax.all_to_all(line_terms, 'dp', 0, 0, tiled=True)]
    unnamed x8 -> x6, local copies, waits for them, and re-layouts: 2.04 us -> 0.71 us
    pallas_call x2 -> x1, Pallas kernels: 3.57 us -> 2.95 us  [final(): pl.pallas_call(functools.partial(final_kernel, full_width, scale=scale),...]
  transfers between devices with their start and end apart: 4 -> 3, of which waited for: 1 -> 1; matrix products, arithmetic and copies ran while one was open for 1% -> 1% of each run, Pallas kernels for 4% -> 0%
where the time goes in v4:
time: 68.9 us; the launch traced here: 68.5 us
  blocking collectives  32.5 us (47%)
  starting transfers between devices  19.9 us (29%)
  Pallas kernels  13.6 us (20%)
  local copies, waits for them, and re-layouts  1.33 us (2%)
    psum x1, blocking collectives, shards(): line_terms = jnp.broadcast_to(lax.psum(term, 'group'), (lines, 1, HD))  19.2 us
    ppermute x1, starting transfers between devices, shards(): arrived = lax.ppermute(pack, 'dp', [(i, i - 1) for i in range(1, lines)])  8.77 us
    all_to_all x1, starting transfers between devices, shards(): terms = lax.all_to_all(line_terms, 'dp', 0, 0, tiled=True)  8.53 us
    pallas_call x1, Pallas kernels, main_part(): pl.pallas_call(functools.partial(main_kernel, full_width), grid=(heads //...  8.46 us
    psum x1, blocking collectives, shards(): squares_all = lax.psum(local_squares, 'tensor')  6.72 us
    psum x1, blocking collectives, shards(): projects_all = lax.psum(project, 'tensor')  6.6 us
    pallas_call x1, Pallas kernels, final(): pl.pallas_call(functools.partial(final_kernel, full_width, scale=scale),...  2.95 us
    ppermute x1, starting transfers between devices, shards(): returned = lax.ppermute(back, 'dp', [(i, i + 1) for i in range(lines - 1)])  2.56 us
  transfers between devices with their start and end apart: 3, of which 1 were waited for; matrix products, arithmetic and copies ran while one was open for 1% of the time, Pallas kernels for 0%

profile of v4, /device:TPU:1, one launch (start us, length us, event | category | flops | bytes accessed | tf_op | source)
XLA Modules:
  0.0 68.5 jit_solution(9361201543249802272)
XLA Ops:
  0.6 2.2 %shard_map.110 = (f32[4,128]{1,0:T(4,128)}, bf16[128,1024]{1,0:T(8,128)(2,1)}) custom-call(bf16[512,1024]{1,0:T(8,128)(2,1)} %x_ref.5, bf16[128,1024]{1,0:T(8,128)(2,1)} %q_ref.3, bf16[128,1024]{1,0:T(8,128)(2,1)} %o_ref.3), custom_call_target="tpu_custom_call" | custom-call | flops 1048576 | bytes 1048576 | tf_op jit(solution)/shard_map/pallas_call | solution.py:72
  2.8 8.8 %collective-permute-start = (bf16[128,1024]{1,0:T(8,128)(2,1)}, bf16[128,1024]{1,0:T(8,128)(2,1)S(1)}, u32[]{:S(2)}, u32[]{:S(2)}) collective-permute-start(bf16[128,1024]{1,0:T(8,128)(2,1)} %get-tuple-element.21), channel_id=1, source_target_pairs={{4,0},{8,4},{12,8},{16,12},{20,16},{24,20},{28,24},{32,28},{36,32}... | collective-permute-start | bytes 786440 | tf_op jit(solution)/shard_map/ppermute | solution.py:401
  11.6 6.7 %psum.23.square_ref = f32[4,128]{1,0:T(4,128)} all-reduce(f32[4,128]{1,0:T(4,128)} %get-tuple-element.20), channel_id=1, replica_groups=mesh['group'=4,'dp'=32,'tensor'=4] {'tensor'}, use_global_device_ids=true, to_apply=%region_0.0 | all-reduce | flops 512 | bytes 4096 | tf_op jit(solution)/shard_map/psum | solution.py:400
  18.3 0.0 collective-permute-done.next_q_ref.next_o_ref
  18.3 0.0 copy-start.2
  18.3 0.7 %copy-done.2 = bf16[128,1024]{1,0:T(8,128)(2,1)} copy-done((bf16[128,1024]{1,0:T(8,128)(2,1)}, bf16[128,1024]{1,0:T(8,128)(2,1)S(1)}, u32[]{:S(2)}) %copy-start.2) | copy-done | bytes 262168
  19.0 0.0 copy-start
  19.0 0.0 copy-start.1
  19.0 8.5 %shard_map.111 = (f32[512,1024]{1,0:T(8,128)}, bf16[128,1024]{1,0:T(8,128)(2,1)}, bf16[128,1024]{1,0:T(8,128)(2,1)}, bf16[128,1024]{1,0:T(8,128)(2,1)}, bf16[128...) custom-call(s32[1,64]{1,0:T(1,128)} %counts_ref.1, f32[8]{0:T(128)} %gate_ref.1, f32[4,128]{1,0:T(4,128)} %psum.23.square_ref, ...), custom_call_target="tpu_custom_call" | custom-call | flops 8000000000 | bytes 10000000 | tf_op jit(solution)/shard_map/pallas_call | solution.py:272
  27.5 2.6 %collective-permute-start.1 = (bf16[128,1024]{1,0:T(8,128)(2,1)}, bf16[128,1024]{1,0:T(8,128)(2,1)S(1)}, u32[]{:S(2)}, u32[]{:S(2)}) collective-permute-start(bf16[128,1024]{1,0:T(8,128)(2,1)} %get-tuple-element.28), channel_id=1, source_target_pairs={{0,4},{4,8},{8,12},{12,16},{16,20},{20,24},{24,28},{28,32},{32,36}... | collective-permute-start | bytes 786440 | tf_op jit(solution)/shard_map/ppermute | solution.py:406
  30.1 19.2 %psum.25 = f32[128]{0:T(128)S(1)} all-reduce(f32[128]{0:T(128)} %bitcast.7), channel_id=1, replica_groups=mesh['group'=4,'dp'=32,'tensor'=4] {'group'}, use_global_device_ids=true, to_apply=%region_1.0 | all-reduce | flops 128 | bytes 1024 | tf_op jit(solution)/shard_map/psum | solution.py:407
  49.2 0.6 broadcast_in_dim.10
  49.9 8.5 %all-to-all-start = ((f32[32,1,128]{2,1,0:T(1,128)}), f32[32,1,128]{2,1,0:T(1,128)S(1)}, u32[]{:S(2)}, u32[]{:S(2)}) async-start(f32[32,1,128]{2,1,0:T(1,128)} %broadcast_in_dim.10), calls=%async_computation | async-start | bytes 32768 | tf_op jit(solution)/shard_map/all_to_all | solution.py:409
  58.4 6.6 %psum.26.project_ref = f32[4,128]{1,0:T(4,128)S(1)} all-reduce(f32[4,128]{1,0:T(4,128)} %get-tuple-element.24), channel_id=1, replica_groups=mesh['group'=4,'dp'=32,'tensor'=4] {'tensor'}, use_global_device_ids=true, to_apply=%region_2.0 | all-reduce | flops 512 | bytes 4096 | tf_op jit(solution)/shard_map/psum | solution.py:410
  65.0 0.5 all-to-all-done.terms_ref
  65.5 0.0 collective-permute-done.1.ret_out_ref.ret_query_ref
  65.5 0.0 copy-done
  65.5 0.0 copy-done.1
  65.5 2.9 %shard_map.112 = (bf16[512,1024]{1,0:T(8,128)(2,1)}, bf16[128,1024]{1,0:T(8,128)(2,1)}, bf16[128,1024]{1,0:T(8,128)(2,1)}, f32[1,8]{1,0:T(1,128)}) custom-call(f32[4,128]{1,0:T(4,128)S(1)} %copy-done, f32[4,128]{1,0:T(4,128)S(1)} %psum.26.project_ref, bf16[512,1024]{1,0:T(8,128)(2,1)} %x_ref.5, ...), custom_call_target="tpu_custom_call", output_to_operand_aliasing={{1}: (4, {}), {2}: (5, {})} | custom-call | flops 2097152 | bytes 4194304 | tf_op jit(solution)/shard_map/pallas_call | solution.py:365
Async XLA Ops:
  2.8 15.5 %collective-permute-start = (bf16[128,1024]{1,0:T(8,128)(2,1)}, bf16[128,1024]{1,0:T(8,128)(2,1)S(1)}, u32[]{:S(2)}, u32[]{:S(2)}) collective-permute-start(bf16[128,1024]{1,0:T(8,128)(2,1)} %get-tuple-element.21), channel_id=1, source_target_pairs={{4,0},{8,4},{12,8},{16,12},{20,16},{24,20},{28,24},{32,28},{36,32}... | collective-permute-start | bytes 786440 | tf_op jit(solution)/shard_map/ppermute | solution.py:401
  18.3 0.7 %copy-start.2 = (bf16[128,1024]{1,0:T(8,128)(2,1)}, bf16[128,1024]{1,0:T(8,128)(2,1)S(1)}, u32[]{:S(2)}) copy-start(bf16[128,1024]{1,0:T(8,128)(2,1)S(1)} %collective-permute-done.next_q_ref.next_o_ref) | copy-start | bytes 786436
  19.0 46.5 %copy-start = (f32[4,128]{1,0:T(4,128)S(1)}, f32[4,128]{1,0:T(4,128)}, u32[]{:S(2)}) copy-start(f32[4,128]{1,0:T(4,128)} %psum.23.square_ref) | copy-start | bytes 6148
  19.0 46.5 %copy-start.1 = (f32[8]{0:T(128)S(1)}, f32[8]{0:T(128)}, u32[]{:S(2)}) copy-start(f32[8]{0:T(128)} %gate_ref.1) | copy-start | bytes 100
  27.5 38.0 %collective-permute-start.1 = (bf16[128,1024]{1,0:T(8,128)(2,1)}, bf16[128,1024]{1,0:T(8,128)(2,1)S(1)}, u32[]{:S(2)}, u32[]{:S(2)}) collective-permute-start(bf16[128,1024]{1,0:T(8,128)(2,1)} %get-tuple-element.28), channel_id=1, source_target_pairs={{0,4},{4,8},{8,12},{12,16},{16,20},{20,24},{24,28},{28,32},{32,36}... | collective-permute-start | bytes 786440 | tf_op jit(solution)/shard_map/ppermute | solution.py:406
  49.9 15.6 %all-to-all-start = ((f32[32,1,128]{2,1,0:T(1,128)}), f32[32,1,128]{2,1,0:T(1,128)S(1)}, u32[]{:S(2)}, u32[]{:S(2)}) async-start(f32[32,1,128]{2,1,0:T(1,128)} %broadcast_in_dim.10), calls=%async_computation | async-start | bytes 32768 | tf_op jit(solution)/shard_map/all_to_all | solution.py:409

commit v5 on v4

--- a/solution.py
+++ b/solution.py
@@ -16,7 +16,7 @@
 EPSILON = 1e-05
 MASKED = -1e30
 VMEM_LIMIT = 60 * 1024 * 1024
-MAIN_LIMIT = 61440 * 1024
+MAIN_LIMIT = 62144 * 1024
 FINAL_LIMIT = 54528 * 1024
 HEADS_PER_STEP = 4
 SIDE_BY_SIDE = 4
@@ -226,7 +226,7 @@
         for k, (i, n) in enumerate(pairs):
             product = gained[k] * scaled[k]
             sums[n] = product if sums[n] is None else sums[n] + product
-            mid_ref[rows[n], cols[i]] = grads[k] + inverse_ref[rows[n], :] * gained[k]
+            mid_ref[rows[n], cols[i]] = (grads[k] + inverse_ref[rows[n], :] * gained[k]).astype(bf16)
             if n % NB == NB - 1:
                 context_grad_ref[n // NB * CH : (n // NB + 1) * CH, cols[i]] = (
                     key_grads[k - 1][NL:, :] + key_grads[k][NL:, :]
@@ -294,7 +294,7 @@
             pl.BlockSpec((1, HD), lambda h: (0, 0)),
         ],
         out_shape=[
-            jax.ShapeDtypeStruct((rows, width), f32),
+            jax.ShapeDtypeStruct((rows, width), bf16),
             token_shape,
             token_shape,
             token_shape,
@@ -341,7 +341,7 @@
         for at in range(0, width, HD):
             cols = slice(at, at + HD)
             x = x_ref[rows, cols].astype(f32)
-            grad_ref[rows, cols] = (mid_ref[rows, cols] - x * factor).astype(bf16)
+            grad_ref[rows, cols] = (mid_ref[rows, cols].astype(f32) - x * factor).astype(bf16)
     last = lax.broadcasted_iota(jnp.int32, (CH, out_ref.shape[1]), 0) == CH - 1
     for own, back, target in (
         (out_in_ref, ret_out_ref, out_ref),

time: 68.9 us -> 69.7 us (1.012)
  local copies, waits for them, and re-layouts: 1.33 us -> 2.65 us
    unnamed x6 -> x12, local copies, waits for them, and re-layouts: 0.71 us -> 2.03 us
where the time goes in v5:
time: 69.7 us; the launch traced here: 69.2 us
  blocking collectives  32.2 us (46%)
  starting transfers between devices  20.1 us (29%)
  Pallas kernels  13.1 us (19%)
  local copies, waits for them, and re-layouts  2.65 us (4%)
    psum x1, blocking collectives, shards(): line_terms = jnp.broadcast_to(lax.psum(term, 'group'), (lines, 1, HD))  19.1 us
    ppermute x1, starting transfers between devices, shards(): arrived = lax.ppermute(pack, 'dp', [(i, i - 1) for i in range(1, lines)])  8.91 us
    all_to_all x1, starting transfers between devices, shards(): terms = lax.all_to_all(line_terms, 'dp', 0, 0, tiled=True)  8.62 us
    pallas_call x1, Pallas kernels, main_part(): pl.pallas_call(functools.partial(main_kernel, full_width), grid=(heads //...  8.2 us
    psum x1, blocking collectives, shards(): projects_all = lax.psum(project, 'tensor')  6.6 us
    psum x1, blocking collectives, shards(): squares_all = lax.psum(local_squares, 'tensor')  6.58 us
    pallas_call x1, Pallas kernels, final(): pl.pallas_call(functools.partial(final_kernel, full_width, scale=scale),...  2.66 us
    ppermute x1, starting transfers between devices, shards(): returned = lax.ppermute(back, 'dp', [(i, i + 1) for i in range(lines - 1)])  2.56 us
  transfers between devices with their start and end apart: 3, of which 1 were waited for; matrix products, arithmetic and copies ran while one was open for 1% of the time, Pallas kernels for 0%

profile of v5, /device:TPU:1, one launch (start us, length us, event | category | flops | bytes accessed | tf_op | source)
XLA Modules:
  0.0 69.2 jit_solution(4054172709882211538)
XLA Ops:
  0.6 2.2 %shard_map.110 = (f32[4,128]{1,0:T(4,128)}, bf16[128,1024]{1,0:T(8,128)(2,1)}) custom-call(bf16[512,1024]{1,0:T(8,128)(2,1)} %x_ref.5, bf16[128,1024]{1,0:T(8,128)(2,1)} %q_ref.3, bf16[128,1024]{1,0:T(8,128)(2,1)} %o_ref.3), custom_call_target="tpu_custom_call" | custom-call | flops 1048576 | bytes 1048576 | tf_op jit(solution)/shard_map/pallas_call | solution.py:72
  2.8 0.0 copy-start.3
  2.8 8.9 %collective-permute-start = (bf16[128,1024]{1,0:T(8,128)(2,1)}, bf16[128,1024]{1,0:T(8,128)(2,1)S(1)}, u32[]{:S(2)}, u32[]{:S(2)}) collective-permute-start(bf16[128,1024]{1,0:T(8,128)(2,1)} %get-tuple-element.21), channel_id=1, source_target_pairs={{4,0},{8,4},{12,8},{16,12},{20,16},{24,20},{28,24},{32,28},{36,32}... | collective-permute-start | bytes 786440 | tf_op jit(solution)/shard_map/ppermute | solution.py:401
  11.7 0.0 copy-done.3
  11.8 6.6 %psum.23.square_ref = f32[4,128]{1,0:T(4,128)} all-reduce(f32[4,128]{1,0:T(4,128)S(1)} %copy-done.3), channel_id=1, replica_groups=mesh['group'=4,'dp'=32,'tensor'=4] {'tensor'}, use_global_device_ids=true, to_apply=%region_0.0 | all-reduce | flops 512 | bytes 4096 | tf_op jit(solution)/shard_map/psum | solution.py:400
  18.3 0.0 collective-permute-done.next_q_ref.next_o_ref
  18.3 0.0 copy-start.4
  18.3 0.7 %copy-done.4 = bf16[128,1024]{1,0:T(8,128)(2,1)} copy-done((bf16[128,1024]{1,0:T(8,128)(2,1)}, bf16[128,1024]{1,0:T(8,128)(2,1)S(1)}, u32[]{:S(2)}) %copy-start.4) | copy-done | bytes 262168
  19.0 8.2 %shard_map.111 = (bf16[512,1024]{1,0:T(8,128)(2,1)}, bf16[128,1024]{1,0:T(8,128)(2,1)}, bf16[128,1024]{1,0:T(8,128)(2,1)}, bf16[128,1024]{1,0:T(8,128)(2,1)}, bf...) custom-call(s32[1,64]{1,0:T(1,128)} %counts_ref.1, f32[8]{0:T(128)} %gate_ref.1, ...), custom_call_target="tpu_custom_call" | custom-call | flops 8000000000 | bytes 10000000 | tf_op jit(solution)/shard_map/pallas_call | solution.py:272
  27.2 2.6 %collective-permute-start.1 = (bf16[128,1024]{1,0:T(8,128)(2,1)}, bf16[128,1024]{1,0:T(8,128)(2,1)S(1)}, u32[]{:S(2)}, u32[]{:S(2)}) collective-permute-start(bf16[128,1024]{1,0:T(8,128)(2,1)} %get-tuple-element.28), channel_id=1, source_target_pairs={{0,4},{4,8},{8,12},{12,16},{16,20},{20,24},{24,28},{28,32},{32,36}... | collective-permute-start | bytes 786440 | tf_op jit(solution)/shard_map/ppermute | solution.py:406
  29.8 0.0 copy-start.5
  29.8 0.6 copy-done.5
  30.5 19.1 %psum.25 = f32[128]{0:T(128)S(1)} all-reduce(f32[128]{0:T(128)S(1)} %bitcast.7), channel_id=1, replica_groups=mesh['group'=4,'dp'=32,'tensor'=4] {'group'}, use_global_device_ids=true, to_apply=%region_1.0 | all-reduce | flops 128 | bytes 1024 | tf_op jit(solution)/shard_map/psum | solution.py:407
  49.5 0.6 broadcast_in_dim.10
  50.2 0.0 copy-start.2
  50.2 8.6 %all-to-all-start = ((f32[32,1,128]{2,1,0:T(1,128)}), f32[32,1,128]{2,1,0:T(1,128)S(1)}, u32[]{:S(2)}, u32[]{:S(2)}) async-start(f32[32,1,128]{2,1,0:T(1,128)} %broadcast_in_dim.10), calls=%async_computation | async-start | bytes 32768 | tf_op jit(solution)/shard_map/all_to_all | solution.py:409
  58.8 0.0 copy-done.2
  58.8 6.6 %psum.26.project_ref = f32[4,128]{1,0:T(4,128)S(1)} all-reduce(f32[4,128]{1,0:T(4,128)S(1)} %copy-done.2), channel_id=1, replica_groups=mesh['group'=4,'dp'=32,'tensor'=4] {'tensor'}, use_global_device_ids=true, to_apply=%region_2.0 | all-reduce | flops 512 | bytes 4096 | tf_op jit(solution)/shard_map/psum | solution.py:410
  65.4 0.5 all-to-all-done.terms_ref
  65.9 0.0 collective-permute-done.1.ret_out_ref.ret_query_ref
  65.9 0.0 copy-start
  65.9 0.0 copy-start.1
  65.9 0.7 copy-done
  66.6 0.0 copy-done.1
  66.6 2.7 %shard_map.112 = (bf16[512,1024]{1,0:T(8,128)(2,1)}, bf16[128,1024]{1,0:T(8,128)(2,1)}, bf16[128,1024]{1,0:T(8,128)(2,1)}, f32[1,8]{1,0:T(1,128)}) custom-call(f32[4,128]{1,0:T(4,128)S(1)} %copy-done, f32[4,128]{1,0:T(4,128)S(1)} %psum.26.project_ref, bf16[512,1024]{1,0:T(8,128)(2,1)} %x_ref.5, ...), custom_call_target="tpu_custom_call", output_to_operand_aliasing={{1}: (4, {}), {2}: (5, {})} | custom-call | flops 2097152 | bytes 4194304 | tf_op jit(solution)/shard_map/pallas_call | solution.py:365
Async XLA Ops:
  2.8 8.9 %copy-start.3 = (f32[4,128]{1,0:T(4,128)S(1)}, f32[4,128]{1,0:T(4,128)}, u32[]{:S(2)}) copy-start(f32[4,128]{1,0:T(4,128)} %get-tuple-element.20) | copy-start | bytes 6148
  2.8 15.5 %collective-permute-start = (bf16[128,1024]{1,0:T(8,128)(2,1)}, bf16[128,1024]{1,0:T(8,128)(2,1)S(1)}, u32[]{:S(2)}, u32[]{:S(2)}) collective-permute-start(bf16[128,1024]{1,0:T(8,128)(2,1)} %get-tuple-element.21), channel_id=1, source_target_pairs={{4,0},{8,4},{12,8},{16,12},{20,16},{24,20},{28,24},{32,28},{36,32}... | collective-permute-start | bytes 786440 | tf_op jit(solution)/shard_map/ppermute | solution.py:401
  18.3 0.7 %copy-start.4 = (bf16[128,1024]{1,0:T(8,128)(2,1)}, bf16[128,1024]{1,0:T(8,128)(2,1)S(1)}, u32[]{:S(2)}) copy-start(bf16[128,1024]{1,0:T(8,128)(2,1)S(1)} %collective-permute-done.next_q_ref.next_o_ref) | copy-start | bytes 786436
  27.2 38.6 %collective-permute-start.1 = (bf16[128,1024]{1,0:T(8,128)(2,1)}, bf16[128,1024]{1,0:T(8,128)(2,1)S(1)}, u32[]{:S(2)}, u32[]{:S(2)}) collective-permute-start(bf16[128,1024]{1,0:T(8,128)(2,1)} %get-tuple-element.28), channel_id=1, source_target_pairs={{0,4},{4,8},{8,12},{12,16},{16,20},{20,24},{24,28},{28,32},{32,36}... | collective-permute-start | bytes 786440 | tf_op jit(solution)/shard_map/ppermute | solution.py:406
  29.8 0.7 copy-start.5
  50.2 8.6 %copy-start.2 = (f32[4,128]{1,0:T(4,128)S(1)}, f32[4,128]{1,0:T(4,128)}, u32[]{:S(2)}) copy-start(f32[4,128]{1,0:T(4,128)} %get-tuple-element.24) | copy-start | bytes 6148
  50.2 15.7 %all-to-all-start = ((f32[32,1,128]{2,1,0:T(1,128)}), f32[32,1,128]{2,1,0:T(1,128)S(1)}, u32[]{:S(2)}, u32[]{:S(2)}) async-start(f32[32,1,128]{2,1,0:T(1,128)} %broadcast_in_dim.10), calls=%async_computation | async-start | bytes 32768 | tf_op jit(solution)/shard_map/all_to_all | solution.py:409
  65.9 0.7 copy-start
  65.9 0.7 copy-start.1
